TPU v7x, 32 devices: a whole 2x2x4 slice. The times are simulated.
32 devices in a mesh: tokens: 8 (over y, x, core), heads: 4 (over z).
Axes of the slice: x: 2, y: 2, z: 4, core: 2. Of those that a mesh axis runs over, the one named last changes fastest.
Arguments:
- inputs: bfloat16 [4096, 2048], P('tokens'), may hold values from -6 to 6
- segments: int32 [4096], P('tokens'), may hold values from 0 to 7, as said below
- pre_gain: bfloat16 [2048], P('tokens'), may hold values from 0.099609375 to 1.8984375
- mid_gain: bfloat16 [2048], P('tokens'), may hold values from 0.099609375 to 1.8984375
- query_weight: bfloat16 [2048, 2048], P('tokens', 'heads'), may hold values from -0.125 to 0.125
- key_weight: bfloat16 [2048, 256], P('tokens', 'heads'), may hold values from -0.125 to 0.125
- value_weight: bfloat16 [2048, 256], P('tokens', 'heads'), may hold values from -0.125 to 0.125
- out_weight: bfloat16 [2048, 2048], P('heads', 'tokens'), may hold values from -0.5 to 0.5
- gate_weight: bfloat16 [2048, 5632], P('tokens', 'heads'), may hold values from -0.125 to 0.125
- up_weight: bfloat16 [2048, 5632], P('tokens', 'heads'), may hold values from -0.125 to 0.125
- down_weight: bfloat16 [5632, 2048], P('heads', 'tokens'), may hold values from -0.109375 to 0.109375
- cotangent: bfloat16 [4096, 2048], P('tokens'), may hold values from -6 to 6
Outputs:
- layer_out: bfloat16 [4096, 2048], P('tokens')
- grad_input: bfloat16 [4096, 2048], P('tokens')
- grad_pre: float32 [2048], P('tokens')
- grad_mid: float32 [2048], P('tokens')
- grad_query: float32 [2048, 2048], P('tokens', 'heads')
- grad_key: float32 [2048, 256], P('tokens', 'heads')
- grad_value: float32 [2048, 256], P('tokens', 'heads')
- grad_out: float32 [2048, 2048], P('heads', 'tokens')
- grad_gate: float32 [2048, 5632], P('tokens', 'heads')
- grad_up: float32 [2048, 5632], P('tokens', 'heads')
- grad_down: float32 [5632, 2048], P('heads', 'tokens')
Inputs may be any that keep to these rules, and one draw needn't show every extreme that they name: `segments`: segment ids never fall and rise by at most 1 from one token to the next; row r holds exactly the four documents 4 r to 4 r + 3, of uneven lengths; in one row drawn from the seed a document begins within the row's first 512 tokens and ends within its last 512.
All inputs are finite; a program needn't handle non-finite values.
Results may differ from a plain program's by a relative error of at most 0.025.
Values may be sent and summed in bfloat16 or wider, within the bound.
A program may use at most 192 MiB of HBM per device.

v0:
```python
import functools
import math

import jax
import jax.numpy as jnp
import numpy as np
from jax import lax
from jax.experimental import pallas as pl
from jax.experimental.pallas import tpu as pltpu
from jax.sharding import PartitionSpec as P

ROW = 2048


def rms_scale(vectors):
    return lax.rsqrt(jnp.mean(vectors * vectors, axis=-1, keepdims=True) + 1e-05)


def rotate(vectors, cos_table, sin_table):
    middle_index = vectors.shape[-1] // 2
    former = vectors[..., :middle_index]
    latter = vectors[..., middle_index:]
    return jnp.concatenate(
        [former * cos_table - latter * sin_table, latter * cos_table + former * sin_table], axis=-1
    )


def unrotate(gradient, cos_table, sin_table):
    middle_index = gradient.shape[-1] // 2
    former = gradient[..., :middle_index]
    latter = gradient[..., middle_index:]
    return jnp.concatenate(
        [former * cos_table + latter * sin_table, latter * cos_table - former * sin_table], axis=-1
    )


def norm_back(gradient, vectors, scale_rows, gain_row):
    shaped = vectors * scale_rows
    weighted = gradient * gain_row
    back_vectors = scale_rows * (
        weighted - shaped * jnp.mean(weighted * shaped, axis=-1, keepdims=True)
    )
    return (back_vectors, jnp.sum(gradient * shaped, axis=0))


def shards_any(
    inputs,
    segments,
    pre_gain,
    mid_gain,
    query_weight,
    key_weight,
    value_weight,
    out_weight,
    gate_weight,
    up_weight,
    down_weight,
    cotangent,
):
    row_count = inputs.shape[0]
    head_size = key_weight.shape[1]
    heads_here = query_weight.shape[1] // head_size
    myself = lax.axis_index("tokens")
    gathered = (
        lax.all_gather(pre_gain, "tokens", axis=0, tiled=True),
        lax.all_gather(mid_gain, "tokens", axis=0, tiled=True),
        lax.all_gather(query_weight, "tokens", axis=0, tiled=True),
        lax.all_gather(key_weight, "tokens", axis=0, tiled=True),
        lax.all_gather(value_weight, "tokens", axis=0, tiled=True),
        lax.all_gather(out_weight, "tokens", axis=1, tiled=True),
        lax.all_gather(gate_weight, "tokens", axis=0, tiled=True),
        lax.all_gather(up_weight, "tokens", axis=0, tiled=True),
        lax.all_gather(down_weight, "tokens", axis=1, tiled=True),
    )
    (
        pre_full,
        mid_full,
        query_full,
        key_full,
        value_full,
        out_full,
        gate_full,
        up_full,
        down_full,
    ) = gathered
    pre_row = pre_full.astype(jnp.float32)
    mid_row = mid_full.astype(jnp.float32)
    all_ids = lax.all_gather(segments, "tokens", axis=0, tiled=True)
    length = all_ids.shape[0]
    places = jnp.arange(length, dtype=jnp.int32)
    starts_here = jnp.concatenate([jnp.ones((1,), dtype=jnp.bool_), all_ids[1:] != all_ids[:-1]])
    opening = lax.cummax(jnp.where(starts_here, places, 0), axis=0)
    own_first = myself * row_count
    positions = lax.dynamic_slice_in_dim(places - opening, own_first, row_count)
    own_places = own_first + jnp.arange(row_count, dtype=jnp.int32)
    half_size = head_size // 2
    inverse = 10000.0 ** (-jnp.arange(half_size, dtype=jnp.float32) / half_size)
    turned = positions.astype(jnp.float32)[:, None] * inverse[None, :]
    cos_table = jnp.cos(turned)[:, None, :]
    sin_table = jnp.sin(turned)[:, None, :]
    inputs_f = inputs.astype(jnp.float32)
    pre_scale = rms_scale(inputs_f)
    normed = (inputs_f * pre_scale * pre_row).astype(jnp.bfloat16)
    queries = jnp.dot(normed, query_full, preferred_element_type=jnp.float32).reshape(
        row_count, heads_here, head_size
    )
    query_rot = (rotate(queries, cos_table, sin_table) * head_size ** (-0.5)).astype(jnp.bfloat16)
    key_rows = jnp.dot(normed, key_full, preferred_element_type=jnp.float32)[:, None, :]
    key_rot = rotate(key_rows, cos_table, sin_table)[:, 0, :].astype(jnp.bfloat16)
    value_low = jnp.dot(normed, value_full, preferred_element_type=jnp.float32).astype(jnp.bfloat16)
    key_all, value_all = (
        lax.all_gather(key_rot, "tokens", axis=0, tiled=True),
        lax.all_gather(value_low, "tokens", axis=0, tiled=True),
    )
    span = math.gcd(ROW, 1024)
    row_start = own_first // ROW * ROW
    block_first = row_start // span
    block_total = (own_first + row_count + span - 1) // span

    def key_block(block_index):
        opening_row = block_index * span
        block_keys = lax.dynamic_slice_in_dim(key_all, opening_row, span)
        block_values = lax.dynamic_slice_in_dim(value_all, opening_row, span)
        block_ids = lax.dynamic_slice_in_dim(all_ids, opening_row, span)
        block_places = opening_row + jnp.arange(span, dtype=jnp.int32)
        allowed = (segments[:, None] == block_ids[None, :]) & (
            own_places[:, None] >= block_places[None, :]
        )
        scores = jnp.einsum(
            "qhd,kd->qhk", query_rot, block_keys, preferred_element_type=jnp.float32
        )
        return (opening_row, block_keys, block_values, allowed[:, None, :], scores)

    def forward_step(block_index, state_now):
        row_peak, row_total, running = state_now
        opening_row, block_keys, block_values, allowed, scores = key_block(block_index)
        new_peak = jnp.maximum(row_peak, jnp.max(jnp.where(allowed, scores, -1e30), axis=-1))
        factor = jnp.exp(row_peak - new_peak)
        weights = jnp.where(allowed, jnp.exp(scores - new_peak[..., None]), 0.0)
        row_total = row_total * factor + jnp.sum(weights, axis=-1)
        running = running * factor[..., None] + jnp.einsum(
            "qhk,kd->qhd",
            weights.astype(jnp.bfloat16),
            block_values,
            preferred_element_type=jnp.float32,
        )
        return (new_peak, row_total, running)

    start_state = (
        jnp.full((row_count, heads_here), -1e30, jnp.float32),
        jnp.zeros((row_count, heads_here), jnp.float32),
        jnp.zeros((row_count, heads_here, head_size), jnp.float32),
    )
    row_peak, row_total, running = lax.fori_loop(
        block_first, block_total, forward_step, start_state
    )
    attended = running / row_total[..., None]
    log_total = row_peak + jnp.log(row_total)
    attended_low = attended.astype(jnp.bfloat16).reshape(row_count, heads_here * head_size)
    attn_term = jnp.dot(attended_low, out_full, preferred_element_type=jnp.float32)
    middle = inputs_f + lax.psum(attn_term.astype(jnp.bfloat16), "heads").astype(jnp.float32)
    mid_scale = rms_scale(middle)
    normed_mid = (middle * mid_scale * mid_row).astype(jnp.bfloat16)
    gate_rows = jnp.dot(normed_mid, gate_full, preferred_element_type=jnp.float32)
    up_rows = jnp.dot(normed_mid, up_full, preferred_element_type=jnp.float32)
    sigmoid_rows = jax.nn.sigmoid(gate_rows)
    silu_rows = gate_rows * sigmoid_rows
    hidden = (silu_rows * up_rows).astype(jnp.bfloat16)
    mlp_term = jnp.dot(hidden, down_full, preferred_element_type=jnp.float32)
    layer_out = (
        middle + lax.psum(mlp_term.astype(jnp.bfloat16), "heads").astype(jnp.float32)
    ).astype(jnp.bfloat16)
    grad_down = jnp.einsum("tf,td->fd", hidden, cotangent, preferred_element_type=jnp.float32)
    back_hidden = jnp.einsum("td,fd->tf", cotangent, down_full, preferred_element_type=jnp.float32)
    back_gate = (
        back_hidden * up_rows * sigmoid_rows * (1.0 + gate_rows * (1.0 - sigmoid_rows))
    ).astype(jnp.bfloat16)
    back_up = (back_hidden * silu_rows).astype(jnp.bfloat16)
    grad_gate = jnp.einsum("tc,tf->cf", normed_mid, back_gate, preferred_element_type=jnp.float32)
    grad_up = jnp.einsum("tc,tf->cf", normed_mid, back_up, preferred_element_type=jnp.float32)
    mid_term = jnp.einsum(
        "tf,cf->tc", back_gate, gate_full, preferred_element_type=jnp.float32
    ) + jnp.einsum("tf,cf->tc", back_up, up_full, preferred_element_type=jnp.float32)
    back_normed_mid = lax.psum(mid_term.astype(jnp.bfloat16), "heads").astype(jnp.float32)
    back_middle, grad_mid = norm_back(back_normed_mid, middle, mid_scale, mid_row)
    back_middle = back_middle + cotangent.astype(jnp.float32)
    back_attn = back_middle.astype(jnp.bfloat16)
    grad_out = jnp.einsum("tc,td->cd", attended_low, back_attn, preferred_element_type=jnp.float32)
    back_attended = (
        jnp.einsum("td,cd->tc", back_attn, out_full, preferred_element_type=jnp.float32)
        .astype(jnp.bfloat16)
        .reshape(row_count, heads_here, head_size)
    )
    row_delta = jnp.sum(back_attended.astype(jnp.float32) * attended, axis=-1)

    def backward_step(block_index, state_now):
        back_rows, back_pairs = state_now
        opening_row, block_keys, block_values, allowed, scores = key_block(block_index)
        chances = jnp.where(allowed, jnp.exp(scores - log_total[..., None]), 0.0)
        back_values = jnp.einsum(
            "qhk,qhd->kd",
            chances.astype(jnp.bfloat16),
            back_attended,
            preferred_element_type=jnp.float32,
        )
        back_chances = jnp.einsum(
            "qhd,kd->qhk", back_attended, block_values, preferred_element_type=jnp.float32
        )
        back_scores = (chances * (back_chances - row_delta[..., None])).astype(jnp.bfloat16)
        back_rows = back_rows + jnp.einsum(
            "qhk,kd->qhd", back_scores, block_keys, preferred_element_type=jnp.float32
        )
        back_keys = jnp.einsum(
            "qhk,qhd->kd", back_scores, query_rot, preferred_element_type=jnp.float32
        )
        old_piece = lax.dynamic_slice_in_dim(back_pairs, opening_row, span)
        fresh_piece = old_piece + jnp.concatenate([back_keys, back_values], axis=-1)
        back_pairs = lax.dynamic_update_slice_in_dim(back_pairs, fresh_piece, opening_row, 0)
        return (back_rows, back_pairs)

    start_back = (
        jnp.zeros((row_count, heads_here, head_size), jnp.float32),
        jnp.zeros((length, 2 * head_size), jnp.float32),
    )
    back_rows, back_pairs = lax.fori_loop(block_first, block_total, backward_step, start_back)
    own_pairs = lax.psum_scatter(
        back_pairs.astype(jnp.bfloat16), "tokens", scatter_dimension=0, tiled=True
    ).astype(jnp.float32)
    back_query = (
        (unrotate(back_rows, cos_table, sin_table) * head_size ** (-0.5))
        .astype(jnp.bfloat16)
        .reshape(row_count, heads_here * head_size)
    )
    back_key = unrotate(own_pairs[:, None, :head_size], cos_table, sin_table)[:, 0, :].astype(
        jnp.bfloat16
    )
    back_value = own_pairs[:, head_size:].astype(jnp.bfloat16)
    grad_query = jnp.einsum("tc,tq->cq", normed, back_query, preferred_element_type=jnp.float32)
    grad_key = jnp.einsum("tc,tq->cq", normed, back_key, preferred_element_type=jnp.float32)
    grad_value = jnp.einsum("tc,tq->cq", normed, back_value, preferred_element_type=jnp.float32)
    pre_term = jnp.einsum("tq,cq->tc", back_query, query_full, preferred_element_type=jnp.float32)
    pre_term = pre_term + jnp.einsum(
        "tq,cq->tc", back_key, key_full, preferred_element_type=jnp.float32
    )
    pre_term = pre_term + jnp.einsum(
        "tq,cq->tc", back_value, value_full, preferred_element_type=jnp.float32
    )
    back_normed = lax.psum(pre_term.astype(jnp.bfloat16), "heads").astype(jnp.float32)
    back_inputs, grad_pre = norm_back(back_normed, inputs_f, pre_scale, pre_row)
    grad_input = (back_middle + back_inputs).astype(jnp.bfloat16)
    summed = (
        lax.psum_scatter(
            grad_pre.astype(jnp.bfloat16), "tokens", scatter_dimension=0, tiled=True
        ).astype(jnp.float32),
        lax.psum_scatter(
            grad_mid.astype(jnp.bfloat16), "tokens", scatter_dimension=0, tiled=True
        ).astype(jnp.float32),
        lax.psum_scatter(
            grad_query.astype(jnp.bfloat16), "tokens", scatter_dimension=0, tiled=True
        ).astype(jnp.float32),
        lax.psum_scatter(
            grad_key.astype(jnp.bfloat16), "tokens", scatter_dimension=0, tiled=True
        ).astype(jnp.float32),
        lax.psum_scatter(
            grad_value.astype(jnp.bfloat16), "tokens", scatter_dimension=0, tiled=True
        ).astype(jnp.float32),
        lax.psum_scatter(
            grad_out.astype(jnp.bfloat16), "tokens", scatter_dimension=1, tiled=True
        ).astype(jnp.float32),
        lax.psum_scatter(
            grad_gate.astype(jnp.bfloat16), "tokens", scatter_dimension=0, tiled=True
        ).astype(jnp.float32),
        lax.psum_scatter(
            grad_up.astype(jnp.bfloat16), "tokens", scatter_dimension=0, tiled=True
        ).astype(jnp.float32),
        lax.psum_scatter(
            grad_down.astype(jnp.bfloat16), "tokens", scatter_dimension=1, tiled=True
        ).astype(jnp.float32),
    )
    (
        grad_pre,
        grad_mid,
        grad_query,
        grad_key,
        grad_value,
        grad_out,
        grad_gate,
        grad_up,
        grad_down,
    ) = summed
    return (
        layer_out,
        grad_input,
        grad_pre,
        grad_mid,
        grad_query,
        grad_key,
        grad_value,
        grad_out,
        grad_gate,
        grad_up,
        grad_down,
    )


MESH_ID = pl.DeviceIdType.MESH
VMEM_BYTES = 63 * 2**20


def token_device(flip):
    return (jnp.bitwise_xor(lax.axis_index("tokens"), flip), lax.axis_index("heads"))


def remote(src, dst, send, recv, device):
    return pltpu.make_async_remote_copy(
        src_ref=src, dst_ref=dst, send_sem=send, recv_sem=recv, device_id=device, device_id_type=MESH_ID
    )


def block_of(ref, axis, index, half=None, part=(0, 1)):
    size = ref.shape[axis] // 8
    start = pl.multiple_of(index * size, size)
    if axis == 0:
        rows = size // part[1]
        start = pl.multiple_of(start + part[0] * rows, rows)
        if half is None:
            return ref.at[pl.ds(start, rows), :]
        rows //= 2
        return ref.at[pl.ds(pl.multiple_of(start + half * rows, rows), rows), :]
    if half is None:
        return ref.at[:, pl.ds(start, size)]
    rows = ref.shape[0] // 2
    return ref.at[pl.ds(half * rows, rows), pl.ds(start, size)]


def in_order(job):
    @pl.when(lax.axis_index("tokens") >= 0)
    def _():
        job()


class Gather:
    COPIES = 9

    def __init__(self, shard, full, axis, send, recv, local, part=(0, 1)):
        self.shard, self.full, self.axis, self.part = shard, full, axis, part
        self.send, self.recv, self.local = send, recv, local
        self.me = lax.axis_index("tokens")

    def copy(self, slot, flip_block, flip_target, half=None):
        index = jnp.bitwise_xor(self.me, flip_block)
        place = block_of(self.full, self.axis, index, half, self.part)
        return remote(
            self.shard if flip_block == 0 else place,
            place,
            self.send.at[slot],
            self.recv.at[slot],
            token_device(flip_target),
        )

    def copies(self, slot):
        return self.copy(
            slot,
            *(
                (0, 2),
                (0, 4),
                (0, 1),
                (2, 4, 0),
                (4, 2, 1),
                (2, 1),
                (4, 1),
                (6, 1, 0),
                (6, 1, 1),
            )[slot],
        )

    def own_copy(self):
        return pltpu.make_async_copy(
            self.shard, block_of(self.full, self.axis, self.me, None, self.part), self.local
        )

    def start(self):
        def job():
            for slot in (0, 1, 2):
                self.copies(slot).start()
            self.own_copy().start()

        in_order(job)

    def relay_x(self):
        def job():
            self.copies(0).wait_recv()
            self.copies(3).start()
            self.copies(5).start()

        in_order(job)

    def relay_y(self):
        def job():
            self.copies(1).wait_recv()
            self.copies(4).start()
            self.copies(6).start()

        in_order(job)

    def relay(self):
        self.relay_x()
        self.relay_y()

    def finish_relay(self):
        def job():
            self.copies(3).wait_recv()
            self.copies(7).start()
            self.copies(4).wait_recv()
            self.copies(8).start()

        in_order(job)

    def finish(self):
        def job():
            for slot in (2, 5, 6, 7, 8):
                self.copies(slot).wait_recv()
            for slot in range(self.COPIES):
                self.copies(slot).wait_send()
            self.own_copy().wait()

        in_order(job)


class LineSum:
    FIRST, SECOND = 1, 3

    def __init__(self, term, passing, total, sems, parts=1):
        self.term, self.passing, self.total, self.sems = term, passing, total, sems
        self.parts, self.blocks = parts, term.shape[0]
        self.count = self.blocks * parts
        here, tokens = lax.axis_index("heads"), lax.axis_index("tokens")
        self.inner = (here == 1) | (here == 2)
        self.mate = (tokens, jnp.where(here < 2, 1 - here, 5 - here))
        self.across = (tokens, jnp.where(self.inner, 3 - here, here))

    def place(self, i):
        rows = self.term.shape[1] // self.parts
        start = multiple(quotient(i, self.blocks) * rows, rows) if self.parts > 1 else 0
        return remainder(i, self.blocks), pl.ds(start, rows)

    def copy(self, src, dst, kind, i, device):
        block, rows = self.place(i)
        return remote(
            src.at[block, rows],
            dst.at[block, rows],
            self.sems.at[kind, i],
            self.sems.at[kind + 1, i],
            device,
        )

    def out_copy(self, i):
        return self.copy(self.term, self.passing, 0, i, self.mate)

    def across_copy(self, i):
        return self.copy(self.passing, self.total, 2, i, self.across)

    def back_copy(self, i):
        return self.copy(self.total, self.total, 4, i, self.mate)

    def add(self, out, other, i):
        block, rows = self.place(i)
        out[block, rows] = (
            out[block, rows].astype(jnp.float32) + other[block, rows].astype(jnp.float32)
        ).astype(out.dtype)

    def due(self, i, who, job):
        if isinstance(i, int):
            if not 0 <= i < self.count:
                return
        else:
            who = who & (i >= 0) & (i < self.count)

        @pl.when(who)
        def _():
            job()

    def step(self, now):
        i, j = now - self.FIRST, now - self.SECOND

        def pass_on():
            self.out_copy(i).wait_recv()
            self.add(self.passing, self.term, i)
            self.across_copy(i).start()

        def settle():
            self.across_copy(j).wait_recv()
            self.add(self.total, self.passing, j)
            self.back_copy(j).start()

        self.due(now, jnp.logical_not(self.inner), lambda: self.out_copy(now).start())
        self.due(i, self.inner, pass_on)
        self.due(j, self.inner, settle)

    def steps(self):
        return self.count + self.SECOND

    def each(self, who, job):
        @pl.when(who)
        def _():
            @pl.loop(0, self.count)
            def _(i):
                job(i)

    def receive(self, i):
        @pl.when(jnp.logical_not(self.inner))
        def _():
            self.back_copy(i).wait_recv()

    def receive_all(self):
        self.each(jnp.logical_not(self.inner), lambda i: self.back_copy(i).wait_recv())

    def finish(self):
        def sent(i):
            self.across_copy(i).wait_send()
            self.back_copy(i).wait_send()

        self.each(self.inner, sent)
        self.each(jnp.logical_not(self.inner), lambda i: self.out_copy(i).wait_send())


def quotient(a, b):
    return a // b if isinstance(a, int) else lax.div(a, b)


def remainder(a, b):
    return a % b if isinstance(a, int) else lax.rem(a, b)


def multiple(value, of):
    return value if isinstance(value, int) else pl.multiple_of(value, of)


def by_step(now, plan):
    for first, last, stride, job in plan:
        if first == last:

            @pl.when(now == first)
            def _():
                job(0)

        else:
            due = (now >= first) & (now <= last)
            if stride > 1:
                due = due & (lax.rem(now - first, stride) == 0)

            @pl.when(due)
            def _():
                job(lax.div(now - first, stride))


def lanes(shape):
    return lax.broadcasted_iota(jnp.int32, shape, len(shape) - 1)


def turn(vectors, cos_table, sin_table):
    near = jnp.where(
        lanes(vectors.shape) % 64 < 32, pltpu.roll(vectors, 96, 1), pltpu.roll(vectors, 32, 1)
    )
    return vectors * cos_table + near * sin_table


def token_column(row):
    return jnp.broadcast_to(row, (128, row.shape[1])).T


def key_marks(column, first_id):
    lane = lanes(column.shape) % 64
    one_hot = (column - first_id).astype(jnp.int32) == lane
    return jnp.where(one_hot | ((lane >= 4) & (lane < 7)), 1.0, 0.0)


def query_marks(column, first_id):
    lane = lanes(column.shape) % 64
    other = (column - first_id).astype(jnp.int32) != lane
    return jnp.where(other & (lane < 4), -1e30, 0.0)


def nt_dot(left, right):
    return lax.dot_general(
        left, right, (((1,), (1,)), ((), ())), preferred_element_type=jnp.float32
    )


def attend_kernel(
    chain, places, x, small, key_shard, value_shard, inverse, query_shard, out_shard, gate_shard, up_shard,
    down_shard, gate_full, up_full, down_full, query_full, pair_full, out_full, attn_sum, normed_out, query_out,
    pairs, attended_out, log_out, cos_out, sin_out, small_out, gate_here, up_here, down_here, small_all, query_here, pair_here, pair_shard,
    out_here, pre_row, normed, query, attended, log_total, cos_table, sin_table, key_side, value_side, marks,
    scores, peak, mixed, near_pairs, term, passing, total, small_sems, gather_sems, local_sems, pair_sems,
    chain_sems, store_sems, load_sems,
):
    count = term.shape[0] // 2
    tokens = x.shape[0]
    heads = query.shape[1] // 64
    me = lax.axis_index("tokens")
    place = lax.rem(me, places)
    far = place >= 2
    loads = [
        pltpu.make_async_copy(src, dst, load_sems.at[k])
        for k, (src, dst) in enumerate(
            ((gate_shard, gate_here), (up_shard, up_here), (down_shard, down_here))
        )
    ]
    for load in loads:
        load.start()
    greet(range(1, 8), chain)

    def small_copy(flip):
        return remote(
            small,
            small_all.at[me],
            small_sems.at[0, flip - 1],
            small_sems.at[1, flip - 1],
            token_device(flip),
        )

    def gather(k, shard, full, axis, part=(0, 1)):
        return Gather(
            shard, full, axis, gather_sems.at[0, k], gather_sems.at[1, k], local_sems.at[k], part
        )

    gather_query = gather(0, query_shard, query_here, 0)
    gather_pair = gather(1, pair_shard, pair_here, 0)
    gather_out = gather(2, out_shard, out_here, 1)
    half_rows = gate_here.shape[0] // 2
    gate_one, gate_two, up, down = (
        gather(3, gate_here.at[pl.ds(0, half_rows)], gate_full, 0, (0, 2)),
        gather(4, gate_here.at[pl.ds(half_rows, half_rows)], gate_full, 0, (1, 2)),
        gather(5, up_here, up_full, 0),
        gather(6, down_here, down_full, 1),
    )
    stores = []

    def store(src, out):
        copy = pltpu.make_async_copy(src, out, store_sems.at[len(stores)])
        copy.start()
        stores.append(copy)

    for flip in range(1, 8):
        small_copy(flip).start()
    both = jnp.concatenate(
        [key_shard[...].astype(jnp.float32), value_shard[...].astype(jnp.float32)], axis=0
    )
    pair_shard[...] = both.T.astype(jnp.bfloat16)
    gather_pair.start()
    gather_query.start()
    small_all[me] = small[...]
    x_f = x[...].astype(jnp.float32)
    pre_scale = lax.rsqrt(jnp.mean(x_f * x_f, axis=1, keepdims=True) + 1e-05)

    for flip in range(1, 8):
        small_copy(flip).wait_recv()
    store(small_all, small_out)
    width = x.shape[1] // 8
    for k in range(8):
        pre_row[:, k * width : (k + 1) * width] = jnp.broadcast_to(
            small_all[k, 1:2, :width], (8, width)
        )
    gather_pair.relay()
    normed[...] = (x[...].astype(jnp.float32) * pre_scale * pre_row[0:1, :]).astype(jnp.bfloat16)
    store(normed, normed_out)
    first_device = me - place
    first_id = (first_device // places * 4).astype(jnp.float32)
    own = token_column(small_all[me, 0:1, :])
    before = jnp.zeros((tokens, 1), jnp.float32)
    for k in range(places):
        others = small_all[first_device + k, 0:1, :]
        before = before + jnp.sum(
            jnp.where(others < own[:, 0:1], 1.0, 0.0), axis=1, keepdims=True
        )
        column = token_column(others)
        marks[pl.ds(k * tokens, tokens), :] = key_marks(column, first_id)
    row_index = lax.broadcasted_iota(jnp.int32, (tokens, 128), 0) + place * tokens
    turned = (row_index.astype(jnp.float32) - before) * inverse[0:1, :]
    cos_table[...] = jnp.cos(turned)
    sin_signed = jnp.sin(turned)
    sin_table[...] = jnp.where(lanes(sin_signed.shape) % 64 < 32, -sin_signed, sin_signed)
    store(cos_table, cos_out)
    store(sin_table, sin_out)
    gather_query.relay()
    gather_pair.finish_relay()
    gather_pair.finish()

    made = jnp.dot(normed[...], pair_here[...], preferred_element_type=jnp.float32)
    spun = turn(made, cos_table[...], sin_table[...])
    near_pairs[place] = jnp.where(lanes(made.shape) < 64, spun, made).astype(jnp.bfloat16)

    def pair_copy(slot, flip):
        at = place - 2 if slot == 2 else place
        return remote(
            near_pairs.at[at],
            near_pairs.at[at],
            pair_sems.at[0, slot],
            pair_sems.at[1, slot],
            token_device(flip),
        )

    pair_copy(0, 1).start()

    @pl.when(jnp.logical_not(far))
    def _():
        pair_copy(1, 2).start()

    gather_out.start()
    for load in loads:
        load.wait()
    gate_one.start()
    gather_query.finish_relay()
    gather_query.finish()
    for low in range(0, query.shape[1], 256):
        made = jnp.dot(
            normed[...], query_here[:, low : low + 256], preferred_element_type=jnp.float32
        )
        for group in range(low, low + 256, 128):
            spun = turn(made[:, group - low : group - low + 128], cos_table[...], sin_table[...])
            query[:, group : group + 128] = (spun * 0.125).astype(jnp.bfloat16)
    store(query, query_out)
    store(query_here, query_full)
    store(pair_here, pair_full)
    pair_copy(0, 1).wait_recv()

    @pl.when(far)
    def _():
        pair_copy(1, 2).wait_recv()
        pair_copy(2, 1).start()
        pair_copy(2, 1).wait_recv()

    @pl.when(jnp.logical_not(far))
    def _():
        gather_out.relay()

    @pl.when(jnp.logical_not(far))
    def _():
        gate_two.start()

    for k in range(places):

        @pl.when(k <= place)
        def _():
            pair = near_pairs[k].astype(jnp.float32)
            swapped = pltpu.roll(pair, 64, 1)
            lane = lanes(pair.shape)
            mark = marks[pl.ds(k * tokens, tokens), :]
            block = pl.ds(k * tokens, tokens)
            key_side[0, block] = jnp.where(lane < 64, pair, mark).astype(jnp.bfloat16)
            key_side[1, block] = jnp.where(lane < 64, mark, swapped).astype(jnp.bfloat16)
            value_side[0, block] = jnp.where(lane < 64, swapped, 1.0).astype(jnp.bfloat16)
            value_side[1, block] = jnp.where(lane < 64, 1.0, pair).astype(jnp.bfloat16)

    store(near_pairs, pairs)
    lane = lanes((tokens, 128))
    own_marks = query_marks(own, first_id)

    def side_of(group, e):
        at = pl.ds(multiple(group * 128, 128), 128)
        mine = (lane < 64) if e == 0 else (lane >= 64)
        return jnp.where(mine, query[:, at].astype(jnp.float32), own_marks).astype(jnp.bfloat16)

    def keys_at(k):
        return pl.ds(pl.multiple_of(k * tokens, tokens), tokens)

    def look(e, side, k, masked):
        found = nt_dot(side, key_side[e, keys_at(k)])
        if masked:
            rows = lax.broadcasted_iota(jnp.int32, found.shape, 0)
            found = jnp.where(lanes(found.shape) <= rows, found, -1e30)
        scores[e, k] = found
        best = found[:, :128]
        for part in range(128, tokens, 128):
            best = jnp.maximum(best, found[:, part : part + 128])
        peak[e] = best if masked else jnp.maximum(peak[e], best)

    def blend(e, k, first):
        parts = [
            jnp.exp(scores[e, k, :, part : part + 128] - peak[e]).astype(jnp.bfloat16)
            for part in range(0, tokens, 128)
        ]
        made = jnp.dot(
            jnp.concatenate(parts, axis=1),
            value_side[e, keys_at(k)],
            preferred_element_type=jnp.float32,
        )
        mixed[e] = made if first else mixed[e] + made

    def settle(e):
        peak[e] = jnp.broadcast_to(jnp.max(peak[e], axis=1, keepdims=True), lane.shape)

    def finish_head(group, e):
        mine = (lane < 64) if e == 0 else (lane >= 64)
        at = pl.ds(multiple(group * 128, 128), 128)
        out = mixed[e]
        sums = jnp.where(mine, pltpu.roll(out, 64, 1), out)
        share = out / sums
        attended[:, at] = share if e == 0 else jnp.where(lane < 64, attended[:, at], share)
        noted = peak[e] + jnp.log(sums)
        log_total[...] = jnp.where(lane == 2 * group + e, noted, log_total[...])

    def stage(done, begun):
        side = side_of(*begun) if begun else None
        if begun:
            look(begun[1], side, place, True)
        if done:
            blend(done[1], place, True)

        @pl.loop(0, place)
        def _(k):
            if begun:
                look(begun[1], side, k, False)
            if done:
                blend(done[1], k, False)

        if done:
            finish_head(*done)
        if begun:
            settle(begun[1])

    log_total[...] = jnp.zeros(lane.shape, jnp.float32)
    stage(None, (0, 0))
    last = heads // 2 - 1

    @pl.loop(0, last)
    def _(group):
        stage((group, 0), (group, 1))

        @pl.when(far & (group == 0))
        def _():
            gather_out.relay()

        @pl.when(far & (group == 0))
        def _():
            gate_two.start()

        @pl.when(group == 2)
        def _():
            up.start()

        stage((group, 1), (group + 1, 0))

    stage((last, 0), (last, 1))
    stage((last, 1), None)
    store(attended, attended_out)
    store(log_total, log_out)
    gather_out.finish_relay()

    gather_out.finish()
    low = attended[...].astype(jnp.bfloat16)
    each = term.shape[2]

    @pl.loop(0, count)
    def _(k):
        cut = pl.ds(pl.multiple_of(k * 2 * each, 2 * each), 2 * each)
        made = jnp.dot(low, out_here[:, cut], preferred_element_type=jnp.float32).astype(
            jnp.bfloat16
        )
        term[2 * k] = made[:, :each]
        term[2 * k + 1] = made[:, each:]

    store(out_here, out_full)

    down.start()
    line = LineSum(term, passing, total, chain_sems, 2)
    relays = [
        (at, at, 1, lambda _, job=job: job())
        for at, job in (
            (0, gate_one.relay),
            (5, gate_two.relay),
            (13, up.relay),
            (24, down.relay),
            (26, gate_one.finish_relay),
            (28, gate_two.finish_relay),
            (32, up.finish_relay),
        )
    ]

    @pl.loop(0, line.steps())
    def _(now):
        by_step(now, relays)
        line.step(now)

    line.receive_all()
    store(total, attn_sum)
    down.finish_relay()
    line.finish()
    for part in (gate_one, gate_two, up, down):
        part.finish()
    for flip in range(1, 8):
        small_copy(flip).wait_send()
    pair_copy(0, 1).wait_send()

    @pl.when(far)
    def _():
        pair_copy(2, 1).wait_send()

    @pl.when(jnp.logical_not(far))
    def _():
        pair_copy(1, 2).wait_send()

    for copy in stores:
        copy.wait()


def attend(
    chain, places, x, small, key_weight, value_weight, inverse, query_weight, out_weight, gate_weight, up_weight,
    down_weight,
):
    tokens, width = x.shape
    count = 8
    heads_wide = query_weight.shape[1]
    bf16, f32 = jnp.bfloat16, jnp.float32
    row = places * tokens
    each = width // (2 * count)
    anywhere, vmem = pl.BlockSpec(memory_space=pl.ANY), pl.BlockSpec(memory_space=pltpu.VMEM)
    shape = jax.ShapeDtypeStruct
    chunks = (2 * count, tokens, each)
    out_shape = [
        shape((gate_weight.shape[0] * 8, gate_weight.shape[1]), bf16),
        shape((up_weight.shape[0] * 8, up_weight.shape[1]), bf16),
        shape((down_weight.shape[0], down_weight.shape[1] * 8), bf16),
        shape((width, heads_wide), bf16),
        shape((width, 128), bf16),
        shape((heads_wide, width), bf16),
        shape(chunks, bf16),
        shape((tokens, width), bf16),
        shape((tokens, heads_wide), bf16),
        shape((places, tokens, 128), bf16),
        shape((tokens, heads_wide), f32),
        shape((tokens, 128), f32),
        shape((tokens, 128), f32),
        shape((tokens, 128), f32),
        shape((8,) + small.shape, f32),
    ]
    return pl.pallas_call(
        functools.partial(attend_kernel, chain, places),
        out_shape=out_shape,
        in_specs=[vmem] * 5 + [anywhere] * 5,
        out_specs=[anywhere] * len(out_shape),
        scratch_shapes=[
            pltpu.VMEM(gate_weight.shape, bf16),
            pltpu.VMEM(up_weight.shape, bf16),
            pltpu.VMEM(down_weight.shape, bf16),
            pltpu.VMEM((8,) + small.shape, f32),
            pltpu.VMEM((width, heads_wide), bf16),
            pltpu.VMEM((width, 128), bf16),
            pltpu.VMEM((width // 8, 128), bf16),
            pltpu.VMEM((heads_wide, width), bf16),
            pltpu.VMEM((8, width), f32),
            pltpu.VMEM((tokens, width), bf16),
            pltpu.VMEM((tokens, heads_wide), bf16),
            pltpu.VMEM((tokens, heads_wide), f32),
            pltpu.VMEM((tokens, 128), f32),
            pltpu.VMEM((tokens, 128), f32),
            pltpu.VMEM((tokens, 128), f32),
            pltpu.VMEM((2, row, 128), bf16),
            pltpu.VMEM((2, row, 128), bf16),
            pltpu.VMEM((row, 128), f32),
            pltpu.VMEM((2, places, tokens, tokens), f32),
            pltpu.VMEM((2, tokens, 128), f32),
            pltpu.VMEM((2, tokens, 128), f32),
            pltpu.VMEM((places, tokens, 128), bf16),
            pltpu.VMEM(chunks, bf16),
            pltpu.VMEM(chunks, bf16),
            pltpu.VMEM(chunks, bf16),
            pltpu.SemaphoreType.DMA((2, 7)),
            pltpu.SemaphoreType.DMA((2, 7, Gather.COPIES)),
            pltpu.SemaphoreType.DMA((7,)),
            pltpu.SemaphoreType.DMA((2, 3)),
            pltpu.SemaphoreType.DMA((6, 4 * count)),
            pltpu.SemaphoreType.DMA((len(out_shape),)),
            pltpu.SemaphoreType.DMA((3,)),
        ],
        compiler_params=pltpu.CompilerParams(
            collective_id=0, has_side_effects=True, vmem_limit_bytes=VMEM_BYTES
        ),
        name="attend_forward",
    )(
        x, small, key_weight.T, value_weight.T, inverse, query_weight, out_weight, gate_weight, up_weight,
        down_weight,
    )


def greet(flips, chain):
    me, here = lax.axis_index("tokens"), lax.axis_index("heads")
    barrier = pltpu.get_barrier_semaphore()
    for flip in flips:
        pl.semaphore_signal(barrier, inc=1, device_id=token_device(flip), device_id_type=MESH_ID)
    for step in (-1, 1):
        near = here + step

        @pl.when((near >= 0) & (near < chain))
        def _():
            pl.semaphore_signal(barrier, inc=1, device_id=(me, near), device_id_type=MESH_ID)

    edge = (here == 0) | (here == chain - 1)

    @pl.when(edge)
    def _():
        pl.semaphore_wait(barrier, len(flips) + 1)

    @pl.when(jnp.logical_not(edge))
    def _():
        pl.semaphore_wait(barrier, len(flips) + 2)


class Reduce:
    COPIES = 6

    def __init__(self, own, near, sems):
        self.own, self.near, self.sems = own, near, sems

    def copy(self, slot):
        k, half, flip = ((1, 0, 2), (3, 0, 2), (2, 1, 4), (3, 1, 4), (2, 0, 4), (1, 1, 2))[slot]
        rows = self.own.shape[1] // 2
        return remote(
            self.own.at[k, pl.ds(half * rows, rows)],
            self.near.at[slot],
            self.sems.at[0, slot],
            self.sems.at[1, slot],
            token_device(flip),
        )

    def put(self, k, block):
        self.own[k] = block.astype(self.own.dtype)
        self.send(k)

    def send(self, k):
        for which, slots in ((3, (1, 3)), (1, (0,)), (2, (2,))):

            @pl.when(k == which)
            def _():
                for slot in slots:
                    self.copy(slot).start()

    def add_near(self, k, half, slot):
        rows = self.own.shape[1] // 2

        @pl.loop(0, rows // 32)
        def _(i):
            here = pl.ds(pl.multiple_of(i * 32, 32), 32)
            place = pl.ds(pl.multiple_of(half * rows + i * 32, 32), 32)
            self.own[k, place] = (
                self.own[k, place].astype(jnp.float32) + self.near[slot, here].astype(jnp.float32)
            ).astype(self.own.dtype)

    def second(self):
        self.copy(1).wait_recv()
        self.add_near(2, 0, 1)
        self.copy(4).start()
        self.copy(3).wait_recv()
        self.add_near(1, 1, 3)
        self.copy(5).start()

    def finish(self, out):
        rows = self.own.shape[1] // 2
        for half, slots in ((0, (0, 4)), (1, (2, 5))):
            for slot in slots:
                self.copy(slot).wait_recv()

            @pl.loop(0, rows // 32)
            def _(i):
                here = pl.ds(pl.multiple_of(i * 32, 32), 32)
                place = pl.ds(pl.multiple_of(half * rows + i * 32, 32), 32)
                total = self.own[0, place].astype(jnp.float32)
                for slot in slots:
                    total = total + self.near[slot, here].astype(jnp.float32)
                out[place, :] = total

        for slot in range(self.COPIES):
            self.copy(slot).wait_send()


def block_order(i):
    return jnp.where(i == 0, 3, jnp.where(i == 1, 1, jnp.where(i == 2, 2, 0)))


def tn_dot(left, right):
    return lax.dot_general(
        left, right, (((0,), (0,)), ((), ())), preferred_element_type=jnp.float32
    )


def tiles_of(length, size):
    return [(low, min(low + size, length)) for low in range(0, length, size)]


def feed_kernel(
    chain, small_all, x_in, attn_in, cotangent_in, gate_full, up_full, down_full, back_sum, hidden_out, mlp_term,
    scale_out, grad_gate_out, grad_up_out, x, attn_sum, cotangent, hidden, scale, grad_gate, grad_up, gate, up, down, mid_row, normed, back_gate, back_up, term, passing, total,
    own_gate, near_gate, own_up, near_up, load_sems, swap_sems, chain_sems, reduce_sems, store_sems,
):
    count = term.shape[0] // 2
    each = term.shape[2]
    tokens, width = x.shape
    inner = gate.shape[1]
    me = lax.axis_index("tokens")
    tiles = tiles_of(inner, 512)
    early = [
        pltpu.make_async_copy(src, dst, load_sems.at[4, k])
        for k, (src, dst) in enumerate(((x_in, x), (attn_in, attn_sum), (cotangent_in, cotangent)))
    ]
    loads = []
    for k, (low, high) in enumerate(tiles):
        cut = pl.ds(low, high - low)
        loads.append(
            (
                pltpu.make_async_copy(gate_full.at[:, cut], gate.at[:, cut], load_sems.at[0, k]),
                pltpu.make_async_copy(up_full.at[:, cut], up.at[:, cut], load_sems.at[1, k]),
                pltpu.make_async_copy(down_full.at[cut, :], down.at[cut, :], load_sems.at[2, k]),
            )
        )
    for load in early:
        load.start()
    for group in loads:
        for load in group:
            load.start()
    greet((1, 2, 4), chain)

    span = width // 8
    for k in range(8):
        mid_row[:, k * span : (k + 1) * span] = jnp.broadcast_to(
            small_all[k, 1:2, span : 2 * span], (8, span)
        )

    early[0].wait()
    early[1].wait()
    line = LineSum(term, passing, total, chain_sems, 2)
    half = tokens // 2

    def swap(k, ref, row, cut):
        return remote(
            ref.at[pl.ds(multiple(row, half), half), cut],
            ref.at[pl.ds(multiple(tokens + row, half), half), cut],
            swap_sems.at[0, k],
            swap_sems.at[1, k],
            token_device(1),
        )

    def swaps_of(part):
        row = part * half
        found = [swap(part, normed, row, pl.ds(0, width))]
        for k, (low, high) in enumerate(tiles):
            for j, ref in enumerate((back_gate, back_up)):
                found.append(
                    swap(2 + (part * len(tiles) + k) * 2 + j, ref, row, pl.ds(low, high - low))
                )
        return found

    def mid_pair(n, row, rows):
        cut = pl.ds(pl.multiple_of(n * 2 * each, 2 * each), 2 * each)
        place = pl.ds(row, rows)
        made = nt_dot(back_gate[place, :], gate[cut, :]) + nt_dot(back_up[place, :], up[cut, :])
        made = made.astype(jnp.bfloat16)
        term[2 * n, place] = made[:, :each]
        term[2 * n + 1, place] = made[:, each:]

    early[2].wait()

    @pl.loop(0, 2)
    def _(part):
        row = pl.multiple_of(part * half, half)
        rows = pl.ds(row, half)

        def middle_here(c):
            cut = slice(c * each, (c + 1) * each)
            return x[rows, cut].astype(jnp.float32) + attn_sum[c, rows].astype(jnp.float32)

        squares = jnp.zeros((half, each), jnp.float32)
        for c in range(2 * count):
            found = middle_here(c)
            squares = squares + found * found
        mid_scale = lax.rsqrt(jnp.sum(squares, axis=1, keepdims=True) / width + 1e-05)
        scale[rows] = jnp.broadcast_to(mid_scale, (half, scale.shape[1]))
        for c in range(2 * count):
            cut = slice(c * each, (c + 1) * each)
            normed[rows, cut] = (middle_here(c) * mid_scale * mid_row[0:1, cut]).astype(jnp.bfloat16)
        copies = swaps_of(part)
        copies[0].start()
        for k, (low, high) in enumerate(tiles):

            @pl.when(part == 0)
            def _():
                for load in loads[k]:
                    load.wait()

            gate_rows = jnp.dot(
                normed[rows, :], gate[:, low:high], preferred_element_type=jnp.float32
            )
            up_rows = jnp.dot(normed[rows, :], up[:, low:high], preferred_element_type=jnp.float32)
            back_hidden = nt_dot(cotangent[rows, :], down[low:high, :])
            sigmoid = jax.nn.sigmoid(gate_rows)
            silu = gate_rows * sigmoid
            hidden[rows, low:high] = (silu * up_rows).astype(jnp.bfloat16)
            back_gate[rows, low:high] = (
                back_hidden * up_rows * sigmoid * (1.0 + gate_rows * (1.0 - sigmoid))
            ).astype(jnp.bfloat16)
            back_up[rows, low:high] = (back_hidden * silu).astype(jnp.bfloat16)
            for copy in copies[1 + 2 * k : 3 + 2 * k]:
                copy.start()

            @pl.when(part == 1)
            def _():
                line.step(2 * k)
                line.step(2 * k + 1)

        @pl.when(part == 0)
        def _():
            @pl.loop(0, count)
            def _(n):
                mid_pair(n, 0, half)

    stores = []

    def store(src, out):
        copy = pltpu.make_async_copy(src, out, store_sems.at[len(stores)])
        copy.start()
        stores.append(copy)

    store(hidden, hidden_out)
    store(scale, scale_out)

    def mlp_place(n):
        rows = pl.ds(pl.multiple_of(lax.rem(n, 4) * tokens, tokens), tokens)
        return rows, lax.div(n, 4) * 2 * each

    def mlp_stores(n):
        rows, low = mlp_place(n)
        return [
            pltpu.make_async_copy(
                gate.at[rows, pl.ds(pl.multiple_of(low + k * each, each), each)],
                mlp_term.at[2 * n + k],
                load_sems.at[3, 2 * n + k],
            )
            for k in range(2)
        ]

    def mlp_pair(n):
        cut = pl.ds(pl.multiple_of(n * 2 * each, 2 * each), 2 * each)
        made = jnp.dot(hidden[...], down[:, cut], preferred_element_type=jnp.float32)
        rows, low = mlp_place(n)
        gate[rows, pl.ds(pl.multiple_of(low, 2 * each), 2 * each)] = made.astype(jnp.bfloat16)
        for copy in mlp_stores(n):
            copy.start()

    gate_sum = Reduce(own_gate, near_gate, reduce_sems.at[0])
    up_sum = Reduce(own_up, near_up, reduce_sems.at[1])

    def grad_block(part, ref, k):
        index = jnp.bitwise_xor(me, 2 * k)
        cut = pl.ds(pl.multiple_of(index * span, span), span)
        part.put(k, tn_dot(normed[:, cut], ref[...]))

    def received(which):
        for part in range(2):
            for copy in swaps_of(part)[which]:
                copy.wait_recv()

    begun = 2 * len(tiles)
    plan = (
        (begun, begun, 1, lambda _: received(slice(0, 1))),
        (begun, begun, 1, lambda _: received(slice(1, None, 2))),
        (begun, begun + 3, 1, lambda i: grad_block(gate_sum, back_gate, block_order(i))),
        (begun, begun + count - 1, 1, lambda i: mid_pair(i, half, half)),
        (begun + 4, begun + 4, 1, lambda _: received(slice(2, None, 2))),
        (begun + 4, begun + 7, 1, lambda i: grad_block(up_sum, back_up, block_order(i))),
        (begun + 8, begun + 8, 1, lambda _: gate_sum.second()),
        (begun + 9, begun + 2 * count + 7, 2, mlp_pair),
        (begun + 16, begun + 16, 1, lambda _: up_sum.second()),
    )

    @pl.loop(begun, line.steps())
    def _(now):
        by_step(now, plan)
        line.step(now)

    gate_sum.finish(grad_gate)
    store(grad_gate, grad_gate_out)
    line.receive_all()
    store(total, back_sum)
    up_sum.finish(grad_up)
    store(grad_up, grad_up_out)
    line.finish()
    for part in range(2):
        for copy in swaps_of(part):
            copy.wait_send()

    @pl.loop(0, count)
    def _(n):
        for copy in mlp_stores(n):
            copy.wait()

    for copy in stores:
        copy.wait()


def feed(chain, small_all, x, attn_sum, cotangent, gate_full, up_full, down_full):
    tokens, width = x.shape
    inner = gate_full.shape[1]
    count = attn_sum.shape[0] // 2
    span = width // 8
    bf16, f32 = jnp.bfloat16, jnp.float32
    anywhere, vmem = pl.BlockSpec(memory_space=pl.ANY), pl.BlockSpec(memory_space=pltpu.VMEM)
    shape = jax.ShapeDtypeStruct
    tiles = len(tiles_of(inner, 512))
    return pl.pallas_call(
        functools.partial(feed_kernel, chain),
        out_shape=[
            shape(attn_sum.shape, bf16),
            shape((tokens, inner), bf16),
            shape(attn_sum.shape, bf16),
            shape((tokens, 128), f32),
            shape((span, inner), f32),
            shape((span, inner), f32),
        ],
        in_specs=[vmem] + [anywhere] * 6,
        out_specs=[anywhere] * 6,
        scratch_shapes=[
            pltpu.VMEM((tokens, width), bf16),
            pltpu.VMEM(attn_sum.shape, bf16),
            pltpu.VMEM((tokens, width), bf16),
            pltpu.VMEM((tokens, inner), bf16),
            pltpu.VMEM((tokens, 128), f32),
            pltpu.VMEM((span, inner), f32),
            pltpu.VMEM((span, inner), f32),
            pltpu.VMEM((width, inner), bf16),
            pltpu.VMEM((width, inner), bf16),
            pltpu.VMEM((inner, width), bf16),
            pltpu.VMEM((8, width), f32),
            pltpu.VMEM((2 * tokens, width), bf16),
            pltpu.VMEM((2 * tokens, inner), bf16),
            pltpu.VMEM((2 * tokens, inner), bf16),
            pltpu.VMEM(attn_sum.shape, bf16),
            pltpu.VMEM(attn_sum.shape, bf16),
            pltpu.VMEM(attn_sum.shape, bf16),
            pltpu.VMEM((4, span, inner), bf16),
            pltpu.VMEM((6, span // 2, inner), bf16),
            pltpu.VMEM((4, span, inner), bf16),
            pltpu.VMEM((6, span // 2, inner), bf16),
            pltpu.SemaphoreType.DMA((5, max(tiles, 2 * count))),
            pltpu.SemaphoreType.DMA((2, 2 + 4 * tiles)),
            pltpu.SemaphoreType.DMA((6, 4 * count)),
            pltpu.SemaphoreType.DMA((2, 2, Reduce.COPIES)),
            pltpu.SemaphoreType.DMA((5,)),
        ],
        compiler_params=pltpu.CompilerParams(
            collective_id=1, has_side_effects=True, vmem_limit_bytes=VMEM_BYTES
        ),
        name="feed_forward",
    )(small_all, x, attn_sum, cotangent, gate_full, up_full, down_full)


def split_marks(values, at):
    high = values.astype(jnp.bfloat16).astype(jnp.float32)
    rest = values - high
    middle = rest.astype(jnp.bfloat16).astype(jnp.float32)
    low = rest - middle
    return jnp.where(at == 4, high, jnp.where(at == 5, middle, jnp.where(at == 6, low, 0.0)))


def return_kernel(
    chain, places, small_all, query, pairs, log_total, cos_table, sin_table, scale,
    attended_in, x_in, attn_in, back_sum, query_full, pair_full, out_full, mlp_term, hidden_in, cotangent, normed_in, layer_out, grad_input, grad_down_out,
    grad_query, grad_key, grad_value, grad_out_out, gains, mid_part, grad_down, grad_out, pair_back, grad_in, in_here, out_here, key_side, value_side, query_side, back_side, back_att,
    back_rows, back_keys, back_values, pair_out, pair_near, normed, back_attn, hidden, cotangents, att_low,
    back_all, pre_row, pre_part, gains_near, mlp_sum, mlp_passing, mlp_total, term, passing, total, own_down,
    near_down, own_in, near_in, own_out, near_out, load_sems, swap_sems, pair_sems, gain_sems, chain_sems,
    reduce_sems, store_sems,
):
    count = term.shape[0] // 2
    each = term.shape[2]
    tokens, width = x_in.shape
    span = width // 8
    groups = query.shape[1] // 128
    me = lax.axis_index("tokens")
    place = lax.rem(me, places)
    first_device = me - place
    mine, theirs = pl.ds(0, tokens), pl.ds(tokens, tokens)

    def load(k, src, dst):
        copy = pltpu.make_async_copy(src, dst, load_sems.at[k])
        copy.start()
        return copy

    load_mlp = load(5, mlp_term, mlp_sum)
    load_cot = load(2, cotangent, cotangents.at[mine, :])
    attended = back_rows
    load_attended = load(7, attended_in, attended)

    def back_at(side, c):
        row = multiple(remainder(c, 4) * tokens, tokens)
        return side.at[quotient(c, 4), pl.ds(row, tokens), :]

    def attn_at(c):
        row = multiple(quotient(remainder(c, 4), 2) * tokens, tokens)
        low = multiple(remainder(c, 2) * each, each)
        return own_down.at[quotient(c, 4), pl.ds(row, tokens), pl.ds(low, each)]

    loads = []
    for c in range(2 * count):
        side = key_side if c < count else value_side
        loads.append(load(16 + c, back_sum.at[c], back_at(side, c % count)))
        loads.append(load(16 + 2 * count + c, x_in.at[:, pl.ds(c * each, each)], term.at[c]))
        loads.append(load(16 + 4 * count + c, attn_in.at[c], attn_at(c)))
    load_out = load(0, out_full, out_here)
    heads_wide = query.shape[1]
    load_in = load(1, query_full, in_here.at[:, pl.ds(0, heads_wide)])
    load_pair = load(6, pair_full, in_here.at[:, pl.ds(heads_wide, 128)])
    load_hidden = load(3, hidden_in, hidden.at[mine, :])
    load_normed = load(4, normed_in, normed.at[mine, :])
    greet(range(1, 8), chain)

    def swap(k, ref):
        copy = remote(
            ref.at[mine, :],
            ref.at[theirs, :],
            swap_sems.at[0, k],
            swap_sems.at[1, k],
            token_device(1),
        )
        copy.start()
        return copy

    def gain_copy(which, src, flip):
        other = jnp.bitwise_xor(me, flip)
        return remote(
            src.at[:, pl.ds(pl.multiple_of(other * span, span), span)],
            gains_near.at[me, :, pl.ds(which * span, span)],
            gain_sems.at[0, which, flip - 1],
            gain_sems.at[1, which, flip - 1],
            token_device(flip),
        )

    mlp_line = LineSum(mlp_sum, mlp_passing, mlp_total, chain_sems.at[0])
    load_mlp.wait()
    mlp_line.step(0)
    for k in range(8):
        pre_row[:, k * span : (k + 1) * span] = jnp.broadcast_to(
            small_all[k, 1:2, span : 2 * span], (8, span)
        )
    for copy in loads:
        copy.wait()
    load_cot.wait()

    def hat_at(c):
        return (term[c].astype(jnp.float32) + attn_at(c)[...].astype(jnp.float32)) * scale[...]

    def cut_at(c):
        return pl.ds(multiple(c * each, each), each)

    summed_here = back_keys.at[1]
    summed_here[...] = jnp.zeros(summed_here.shape, jnp.float32)
    for base, side in ((0, key_side), (count, value_side)):

        @pl.loop(0, count)
        def _(c):
            cut = cut_at(base + c)
            shared = back_at(side, c)[...].astype(jnp.float32) * hat_at(base + c)
            summed_here[...] += shared * pre_row[0:1, cut]
            mid_part[:, cut] = jnp.broadcast_to(jnp.sum(shared, axis=0, keepdims=True), (8, each))

    mean = jnp.sum(summed_here[...], axis=1, keepdims=True) / width
    summed_here[...] = jnp.broadcast_to(mean, summed_here.shape)
    for flip in range(1, 8):
        gain_copy(1, mid_part, flip).start()
    mlp_line.step(1)
    for base, side in ((0, key_side), (count, value_side)):

        @pl.loop(0, count)
        def _(c):
            cut = cut_at(base + c)
            u = back_at(side, c)[...].astype(jnp.float32) * pre_row[0:1, cut]
            found = scale[...] * (u - hat_at(base + c) * summed_here[...])
            back_attn[mine, cut] = (cotangents[mine, cut].astype(jnp.float32) + found).astype(
                jnp.bfloat16
            )

    mlp_line.step(2)
    load_attended.wait()
    att_low[mine, :] = attended[...].astype(jnp.bfloat16)
    swap_back = swap(0, back_attn)
    swap_att = swap(1, att_low)

    lane = lanes((tokens, 128))
    at = lane % 64
    first_id = (first_device // places * 4).astype(jnp.float32)
    for k in range(places):
        mark = key_marks(token_column(small_all[first_device + k, 0:1, :]), first_id)
        block = pl.ds(k * tokens, tokens)

        @pl.when(k <= place)
        def _():
            pair = pairs[k].astype(jnp.float32)
            swapped = pltpu.roll(pair, 64, 1)
            key_side[0, block] = jnp.where(lane < 64, pair, mark).astype(jnp.bfloat16)
            key_side[1, block] = jnp.where(lane < 64, mark, swapped).astype(jnp.bfloat16)
            value_side[0, block] = jnp.where(lane < 64, swapped, 1.0).astype(jnp.bfloat16)
            value_side[1, block] = jnp.where(lane < 64, 1.0, pair).astype(jnp.bfloat16)

    own_marks = query_marks(token_column(small_all[me, 0:1, :]), first_id)

    load_out.wait()
    back_att[...] = nt_dot(back_attn[mine, :], out_here[...]).astype(jnp.bfloat16)
    swap_cot = swap(2, cotangents)
    mlp_line.step(3)
    load_hidden.wait()
    swap_hidden = swap(3, hidden)

    @pl.loop(0, groups)
    def _(group):
        cut = pl.ds(pl.multiple_of(group * 128, 128), 128)
        back = back_att[:, cut].astype(jnp.float32)
        both = query[:, cut].astype(jnp.float32)
        shared = back * attended[:, cut]
        for e in range(2):
            head = 2 * group + e
            used = (lane < 64) if e == 0 else (lane >= 64)
            delta = jnp.sum(jnp.where(used, shared, 0.0), axis=1, keepdims=True)
            peak = jnp.sum(jnp.where(lane == head, log_total[...], 0.0), axis=1, keepdims=True)
            back_side[head] = jnp.where(
                used, back, split_marks(jnp.broadcast_to(-delta, lane.shape), at)
            ).astype(jnp.bfloat16)
            query_side[head] = jnp.where(
                used, both, own_marks + split_marks(jnp.broadcast_to(-peak, lane.shape), at)
            ).astype(jnp.bfloat16)

    load_normed.wait()
    swap_normed = swap(4, normed)
    load_in.wait()
    load_pair.wait()

    begun = 4
    back_rows[...] = jnp.zeros_like(back_rows)

    def key_step(k, diagonal):
        back_keys[...] = jnp.zeros_like(back_keys)
        back_values[...] = jnp.zeros_like(back_values)

        @pl.loop(0, groups)
        def _(group):
            cut = pl.ds(pl.multiple_of(group * 128, 128), 128)
            for low in (0, tokens // 2):
                keys_here = pl.ds(pl.multiple_of(k * tokens + low, tokens // 2), tokens // 2)
                part = pl.ds(low, tokens // 2)
                first = low if diagonal else 0
                seen = pl.ds(first, tokens - first)
                rows = []
                for e in range(2):
                    head = 2 * group + e
                    found = nt_dot(key_side[e, keys_here], query_side[head, seen])
                    chances = jnp.exp(found)
                    if diagonal:
                        keys = lax.broadcasted_iota(jnp.int32, found.shape, 0) + (low - first)
                        chances = jnp.where(keys <= lanes(found.shape), chances, 0.0)
                    moved = chances * nt_dot(value_side[e, keys_here], back_side[head, seen])
                    chances = chances.astype(jnp.bfloat16)
                    moved = moved.astype(jnp.bfloat16)
                    back_values[e, part] += jnp.dot(
                        chances, back_att[seen, cut], preferred_element_type=jnp.float32
                    )
                    back_keys[e, part] += jnp.dot(
                        moved, query[seen, cut], preferred_element_type=jnp.float32
                    )
                    rows.append(tn_dot(moved, key_side[e, keys_here]))
                back_rows[seen, cut] += jnp.where(lanes(rows[0].shape) < 64, rows[0], rows[1])

            @pl.when(group % 2 == 1)
            def _():
                mlp_line.step(begun + groups // 2 * k + group // 2)

        keys = back_keys[0] + pltpu.roll(back_keys[1], 64, 1)
        values = pltpu.roll(back_values[0], 64, 1) + back_values[1]
        return jnp.where(lane < 64, keys, values)

    def pair_copy(source, target):
        return remote(
            pair_out.at[target],
            pair_near.at[source],
            pair_sems.at[0, target],
            pair_sems.at[1, source],
            (first_device + target, lax.axis_index("heads")),
        )

    @pl.loop(0, place)
    def _(k):
        pair_out[k] = key_step(k, False).astype(jnp.bfloat16)
        pair_copy(place, k).start()

    own_pair = key_step(place, True)
    pair_out[place] = own_pair.astype(jnp.bfloat16)
    early = begun + groups // 2 * places

    @pl.loop(begun + groups // 2 * (place + 1), early)
    def _(now):
        mlp_line.step(now)

    for group in range(groups):
        cut = slice(group * 128, (group + 1) * 128)
        back_all[mine, cut] = (
            turn(back_rows[:, cut], cos_table[...], -sin_table[...]) * 0.125
        ).astype(jnp.bfloat16)
    back_keys[0] = own_pair
    for k in range(1, places):

        @pl.when(k > place)
        def _():
            remote(
                pair_out.at[k],
                pair_near.at[k],
                pair_sems.at[0, k],
                pair_sems.at[1, k],
                (first_device + k, lax.axis_index("heads")),
            ).wait_recv()
            back_keys[0] += pair_near[k].astype(jnp.float32)

    summed = back_keys[0]
    spun = turn(summed, cos_table[...], -sin_table[...])
    back_all[mine, pl.ds(groups * 128, 128)] = jnp.where(lane < 64, spun, summed).astype(
        jnp.bfloat16
    )
    swap_all = swap(5, back_all)

    def pre_pair(n):
        cut = pl.ds(pl.multiple_of(n * 2 * each, 2 * each), 2 * each)
        made = nt_dot(back_all[mine, :], in_here[cut, :]).astype(jnp.bfloat16)
        term[2 * n] = made[:, :each]
        term[2 * n + 1] = made[:, each:]

    def cut_of(k):
        index = jnp.bitwise_xor(me, 2 * k)
        return pl.ds(pl.multiple_of(index * span, span), span)

    down_sum = Reduce(own_down, near_down, reduce_sems.at[0])
    in_sum = Reduce(own_in, near_in, reduce_sems.at[1])
    out_sum = Reduce(own_out, near_out, reduce_sems.at[2])

    def down_block(i):
        k = block_order(i)
        for low, high in tiles_of(hidden.shape[1], 512):
            own_down[k, low:high] = tn_dot(hidden[:, low:high], cotangents[:, cut_of(k)]).astype(
                own_down.dtype
            )
        down_sum.send(k)

    def in_block(i):
        k = block_order(i)
        in_sum.put(k, tn_dot(normed[:, cut_of(k)], back_all[...]))

    def out_block(i):
        k = block_order(i)
        out_sum.put(k, tn_dot(att_low[...], back_attn[:, cut_of(k)]))

    def late_loads():
        copies = [pltpu.make_async_copy(x_in, cotangents.at[theirs, :], load_sems.at[8])]
        for c in range(2 * count):
            copies.append(
                pltpu.make_async_copy(
                    attn_in.at[c],
                    cotangents.at[mine, pl.ds(c * each, each)],
                    load_sems.at[16 + c],
                )
            )
        return copies

    def load_late():
        swap_cot.wait_send()
        for copy in late_loads():
            copy.start()

    def x_at(c):
        return cotangents[theirs, cut_at(c)].astype(jnp.float32)

    def middle_at(c):
        return x_at(c) + cotangents[mine, cut_at(c)].astype(jnp.float32)

    wholes = (
        (grad_down, grad_down_out),
        (grad_out, grad_out_out),
        (grad_in.at[:, pl.ds(0, heads_wide)], grad_query),
        (pair_back.at[pl.ds(0, 64)], grad_key),
        (pair_back.at[pl.ds(64, 64)], grad_value),
    )

    def whole(k):
        return pltpu.make_async_copy(*wholes[k], store_sems.at[4 * count + k])

    def store_block(c, src, out, first):
        return pltpu.make_async_copy(src.at[c], out.at[:, cut_at(c)], store_sems.at[first + c])

    def finish_mlp(_):
        mlp_line.receive_all()
        mlp_line.finish()

        @pl.loop(0, 2 * count)
        def _(c):
            mlp_sum[c] = (middle_at(c) + mlp_total[c].astype(jnp.float32)).astype(jnp.bfloat16)
            store_block(c, mlp_sum, layer_out, 0).start()

    weighed = back_keys.at[1]
    scale_here = back_keys.at[0]

    def scale_rows(_):
        for copy in late_loads():
            copy.wait()
        for k in range(8):
            pre_row[:, k * span : (k + 1) * span] = jnp.broadcast_to(
                small_all[k, 1:2, :span], (8, span)
            )
        scale_here[...] = jnp.zeros(scale_here.shape, jnp.float32)

        @pl.loop(0, 2 * count)
        def _(c):
            part = x_at(c)
            scale_here[...] += part * part

        mean = jnp.sum(scale_here[...], axis=1, keepdims=True) / width
        scale_here[...] = jnp.broadcast_to(lax.rsqrt(mean + 1e-05), scale_here.shape)
        weighed[...] = jnp.zeros(weighed.shape, jnp.float32)

    def weigh(i):
        line.receive(i)
        c, rows = line.place(i)
        size = tokens // line.parts
        first = lax.div(i, line.blocks) * size
        cut = cut_at(c)
        late = pl.ds(pl.multiple_of(tokens + first, size), size)
        hat = cotangents[late, cut].astype(jnp.float32) * scale_here[rows]
        shared = total[c, rows].astype(jnp.float32) * hat
        weighed[rows] += shared * pre_row[0:1, cut]
        summed = jnp.broadcast_to(jnp.sum(shared, axis=0, keepdims=True), (8, each))
        pre_part[:, cut] = jnp.where(i < line.blocks, 0.0, pre_part[:, cut]) + summed

    def finish_in(_):
        in_sum.finish(grad_in)
        pair_back[...] = grad_in[:, heads_wide:].T
        for k in (2, 3, 4):
            whole(k).start()

    def finish_down(_):
        down_sum.finish(grad_down)
        whole(0).start()

    def finish_out(_):
        out_sum.finish(grad_out)
        whole(1).start()

    line = LineSum(term, passing, total, chain_sems.at[1], 2)
    steps = line.steps()
    behind = 14

    def received(*copies):
        def job(_):
            for copy in copies:
                copy.wait_recv()

        return job

    plan = (
        (0, 2 * count - 2, 2, pre_pair),
        (1, 1, 1, received(swap_cot, swap_hidden)),
        (1, 7, 2, down_block),
        (8, 8, 1, lambda _: load_late()),
        (9, 9, 1, received(swap_back, swap_att)),
        (9, 12, 1, out_block),
        (13, 13, 1, received(swap_normed, swap_all)),
        (13, 13, 1, scale_rows),
        (14, 17, 1, in_block),
        (18, 18, 1, lambda _: down_sum.second()),
        (20, 20, 1, finish_mlp),
        (21, 21, 1, lambda _: out_sum.second()),
        (23, 23, 1, lambda _: in_sum.second()),
        (28, 28, 1, finish_down),
        (30, 30, 1, finish_out),
        (32, 32, 1, finish_in),
    )

    @pl.loop(0, steps)
    def _(now):
        by_step(now, plan)

        @pl.when(early + now < mlp_line.steps())
        def _():
            mlp_line.step(early + now)

        line.step(now)

        @pl.when(now >= behind)
        def _():
            weigh(now - behind)

    @pl.loop(steps - behind, line.count)
    def _(i):
        weigh(i)

    for flip in range(1, 8):
        gain_copy(0, pre_part, flip).start()
    mean = jnp.sum(weighed[...], axis=1, keepdims=True) / width
    weighed[...] = jnp.broadcast_to(mean, weighed.shape)
    line.finish()

    @pl.loop(0, 2 * count)
    def _(c):
        cut = cut_at(c)
        u = total[c].astype(jnp.float32) * pre_row[0:1, cut]
        found = scale_here[...] * (u - x_at(c) * scale_here[...] * weighed[...])
        term[c] = (back_attn[mine, cut].astype(jnp.float32) + found).astype(jnp.bfloat16)
        store_block(c, term, grad_input, 2 * count).start()

    own = pl.ds(pl.multiple_of(me * span, span), span)
    gains_near[me, :, :span] = pre_part[:, own]
    gains_near[me, :, span:] = mid_part[:, own]
    for flip in range(1, 8):
        for which, src in enumerate((pre_part, mid_part)):
            gain_copy(which, src, flip).wait_recv()
    gains[...] = jnp.sum(gains_near[...], axis=0)
    for flip in range(1, 8):
        for which, src in enumerate((pre_part, mid_part)):
            gain_copy(which, src, flip).wait_send()
    for copy in (swap_back, swap_att, swap_hidden, swap_normed, swap_all):
        copy.wait_send()

    @pl.loop(0, place)
    def _(k):
        pair_copy(place, k).wait_send()

    for k in range(len(wholes)):
        whole(k).wait()

    @pl.loop(0, 2 * count)
    def _(c):
        store_block(c, mlp_sum, layer_out, 0).wait()
        store_block(c, term, grad_input, 2 * count).wait()


def way_back(
    chain, places, small_all, query, pairs, log_total, cos_table, sin_table, scale, attended, x, attn_sum, back_sum,
    query_full, pair_full, out_full, mlp_term, hidden, cotangent, normed,
):
    tokens, width = x.shape
    inner = hidden.shape[1]
    heads_wide = query.shape[1]
    wide = heads_wide + 128
    chunks = attn_sum.shape
    count = chunks[0] // 2
    span = width // 8
    row = places * tokens
    bf16, f32 = jnp.bfloat16, jnp.float32
    anywhere, vmem = pl.BlockSpec(memory_space=pl.ANY), pl.BlockSpec(memory_space=pltpu.VMEM)
    shape = jax.ShapeDtypeStruct
    return pl.pallas_call(
        functools.partial(return_kernel, chain, places),
        out_shape=[
            shape((tokens, width), bf16),
            shape((tokens, width), bf16),
            shape((inner, span), f32),
            shape((span, heads_wide), f32),
            shape((64, span), f32),
            shape((64, span), f32),
            shape((heads_wide, span), f32),
            shape((8, 2 * span), f32),
        ],
        in_specs=[vmem] * 7 + [anywhere] * 11,
        out_specs=[anywhere] * 7 + [vmem],
        scratch_shapes=[
            pltpu.VMEM((8, width), f32),
            pltpu.VMEM((inner, span), f32),
            pltpu.VMEM((heads_wide, span), f32),
            pltpu.VMEM((128, span), f32),
            pltpu.VMEM((span, wide), f32),
            pltpu.VMEM((width, wide), bf16),
            pltpu.VMEM((heads_wide, width), bf16),
            pltpu.VMEM((2, row, 128), bf16),
            pltpu.VMEM((2, row, 128), bf16),
            pltpu.VMEM((heads_wide // 64, tokens, 128), bf16),
            pltpu.VMEM((heads_wide // 64, tokens, 128), bf16),
            pltpu.VMEM((tokens, heads_wide), bf16),
            pltpu.VMEM((tokens, heads_wide), f32),
            pltpu.VMEM((2, tokens, 128), f32),
            pltpu.VMEM((2, tokens, 128), f32),
            pltpu.VMEM((places, tokens, 128), bf16),
            pltpu.VMEM((places, tokens, 128), bf16),
            pltpu.VMEM((2 * tokens, width), bf16),
            pltpu.VMEM((2 * tokens, width), bf16),
            pltpu.VMEM((2 * tokens, inner), bf16),
            pltpu.VMEM((2 * tokens, width), bf16),
            pltpu.VMEM((2 * tokens, heads_wide), bf16),
            pltpu.VMEM((2 * tokens, wide), bf16),
            pltpu.VMEM((8, width), f32),
            pltpu.VMEM((8, width), f32),
            pltpu.VMEM((8, 8, 2 * span), f32),
            pltpu.VMEM(chunks, bf16),
            pltpu.VMEM(chunks, bf16),
            pltpu.VMEM(chunks, bf16),
            pltpu.VMEM(chunks, bf16),
            pltpu.VMEM(chunks, bf16),
            pltpu.VMEM(chunks, bf16),
            pltpu.VMEM((4, inner, span), bf16),
            pltpu.VMEM((6, inner // 2, span), bf16),
            pltpu.VMEM((4, span, wide), bf16),
            pltpu.VMEM((6, span // 2, wide), bf16),
            pltpu.VMEM((4, heads_wide, span), bf16),
            pltpu.VMEM((6, heads_wide // 2, span), bf16),
            pltpu.SemaphoreType.DMA((16 + 6 * count,)),
            pltpu.SemaphoreType.DMA((2, 6)),
            pltpu.SemaphoreType.DMA((2, places)),
            pltpu.SemaphoreType.DMA((2, 2, 7)),
            pltpu.SemaphoreType.DMA((2, 6, 4 * count)),
            pltpu.SemaphoreType.DMA((3, 2, Reduce.COPIES)),
            pltpu.SemaphoreType.DMA((4 * count + 5,)),
        ],
        compiler_params=pltpu.CompilerParams(
            collective_id=2, has_side_effects=True, vmem_limit_bytes=VMEM_BYTES
        ),
        name="way_back",
    )(
        small_all, query, pairs, log_total, cos_table, sin_table, scale, attended, x, attn_sum, back_sum,
        query_full, pair_full, out_full, mlp_term, hidden, cotangent, normed,
    )


def hand_over_kernel(count, *refs):
    ins, outs, held = refs[:count], refs[count : 2 * count], refs[2 * count : 3 * count]
    sems = refs[3 * count]
    loads = [pltpu.make_async_copy(ins[k], held[k], sems.at[0, k]) for k in range(count)]
    stores = [pltpu.make_async_copy(held[k], outs[k], sems.at[1, k]) for k in range(count)]
    for load in loads:
        load.start()
    for load, store in zip(loads, stores):
        load.wait()
        store.start()
    for store in stores:
        store.wait()


def hand_over(*arrays):
    count = len(arrays)
    anywhere = pl.BlockSpec(memory_space=pl.ANY)
    return pl.pallas_call(
        functools.partial(hand_over_kernel, count),
        out_shape=[jax.ShapeDtypeStruct(array.shape, array.dtype) for array in arrays],
        in_specs=[anywhere] * count,
        out_specs=[anywhere] * count,
        scratch_shapes=[pltpu.VMEM(array.shape, array.dtype) for array in arrays]
        + [pltpu.SemaphoreType.DMA((2, count))],
        compiler_params=pltpu.CompilerParams(vmem_limit_bytes=VMEM_BYTES),
        name="hand_over",
    )(*arrays)


def shards_cube(
    chain,
    inputs,
    segments,
    pre_gain,
    mid_gain,
    query_weight,
    key_weight,
    value_weight,
    out_weight,
    gate_weight,
    up_weight,
    down_weight,
    cotangent,
):
    row_count = inputs.shape[0]
    head_size = key_weight.shape[1]
    query_width = query_weight.shape[1]
    heads_here = query_width // head_size
    places = ROW // row_count
    half = row_count // 2
    gains = jnp.pad(pre_gain.astype(jnp.float32), (0, half)) + jnp.pad(
        mid_gain.astype(jnp.float32), (half, 0)
    )
    sublane = lax.broadcasted_iota(jnp.int32, (8, row_count), 0)
    small = jnp.where(
        sublane == 0, segments.astype(jnp.float32)[None], jnp.where(sublane == 1, gains[None], 0.0)
    )
    half_size = head_size // 2
    inverse = 10000.0 ** (-np.arange(half_size, dtype=np.float32) / half_size)
    inverse = jnp.asarray(np.tile(inverse.astype(np.float32), (8, 128 // half_size)))
    (
        gate_full,
        up_full,
        down_full,
        query_full,
        pair_full,
        out_full,
        attn_sum,
        normed,
        query_rot,
        pairs,
        attended,
        log_total,
        cos_wide,
        sin_wide,
        small_full,
    ) = attend(
        chain,
        places,
        inputs,
        small,
        key_weight,
        value_weight,
        inverse,
        query_weight,
        out_weight,
        gate_weight,
        up_weight,
        down_weight,
    )
    back_sum, hidden, mlp_term, scale, grad_gate, grad_up = feed(
        chain, small_full, inputs, attn_sum, cotangent, gate_full, up_full, down_full
    )
    layer_out, grad_input, grad_down, grad_query, grad_key, grad_value, grad_out, gains = way_back(
        chain,
        places,
        small_full,
        query_rot,
        pairs,
        log_total,
        cos_wide,
        sin_wide,
        scale,
        attended,
        inputs,
        attn_sum,
        back_sum,
        query_full,
        pair_full,
        out_full,
        mlp_term,
        hidden,
        cotangent,
        normed,
    )
    grad_pre, grad_mid = jnp.split(gains[0], 2)
    layer_out, grad_input, grad_query, grad_key, grad_value, grad_out, grad_gate, grad_up, grad_down = hand_over(
        layer_out, grad_input, grad_query, grad_key, grad_value, grad_out, grad_gate, grad_up, grad_down
    )
    grad_key, grad_value = grad_key.T, grad_value.T
    return (
        layer_out,
        grad_input,
        grad_pre,
        grad_mid,
        grad_query,
        grad_key,
        grad_value,
        grad_out,
        grad_gate,
        grad_up,
        grad_down,
    )


def solution(mesh):
    sizes = dict(mesh.shape)
    plan = shards_any
    if sizes["tokens"] == 8 and sizes["heads"] == 4:
        plan = functools.partial(shards_cube, sizes["heads"])
    return jax.shard_map(
        plan,
        mesh=mesh,
        in_specs=(
            P("tokens", None),
            P("tokens"),
            P("tokens"),
            P("tokens"),
            P("tokens", "heads"),
            P("tokens", "heads"),
            P("tokens", "heads"),
            P("heads", "tokens"),
            P("tokens", "heads"),
            P("tokens", "heads"),
            P("heads", "tokens"),
            P("tokens", None),
        ),
        out_specs=(
            P("tokens", None),
            P("tokens", None),
            P("tokens"),
            P("tokens"),
            P("tokens", "heads"),
            P("tokens", "heads"),
            P("tokens", "heads"),
            P("heads", "tokens"),
            P("tokens", "heads"),
            P("tokens", "heads"),
            P("heads", "tokens"),
        ),
        check_vma=False,
    )
```

profile of v0, /device:TPU:0, one launch (start us, length us, event | category | flops | bytes accessed | tf_op | source)
XLA Modules:
  0.0 323.9 jit_solution(9372150252513462881)
XLA Ops:
  0.7 0.7 convert_element_type.6
  1.3 0.7 convert_add_fusion
  2.0 0.7 select_select_fusion.small
  2.7 105.6 %attend_forward.1 = (bf16[2048,1408]{1,0:T(8,128)(2,1)}, bf16[2048,1408]{1,0:T(8,128)(2,1)}, bf16[1408,2048]{1,0:T(8,128)(2,1)}, bf16[2048,512]{1,0:T(8,128)(2,1...) custom-call(bf16[512,2048]{1,0:T(8,128)(2,1)} %x_in.3, ...), custom_call_target="tpu_custom_call" | custom-call | tf_op jit(solution)/shard_map/attend_forward/pallas_call | solution.py:938
  108.3 84.4 %feed_forward.1 = (bf16[16,512,128]{2,1,0:T(8,128)(2,1)}, bf16[512,1408]{1,0:T(8,128)(2,1)}, bf16[16,512,128]{2,1,0:T(8,128)(2,1)}, f32[512,128]{1,0:T(8,128)}, ...) custom-call(f32[8,8,512]{2,1,0:T(8,128)} %get-tuple-element.49.small_all, bf16[512,2048]{1,0:T(8,128)(2,1)} %x_in.3, ...), custom_call_target="tpu_custom_call" | custom-call | tf_op jit(solution)/shard_map/feed_forward/pallas_call | solution.py:1309
  192.7 122.4 %way_back.1 = (bf16[512,2048]{1,0:T(8,128)(2,1)}, bf16[512,2048]{1,0:T(8,128)(2,1)}, f32[1408,256]{1,0:T(8,128)}, f32[256,512]{1,0:T(8,128)}, f32[64,256]{1,0:T(...) custom-call(f32[8,8,512]{2,1,0:T(8,128)} %get-tuple-element.49.small_all, ...), custom_call_target="tpu_custom_call" | custom-call | tf_op jit(solution)/shard_map/way_back/pallas_call | solution.py:1853
  315.1 7.4 %hand_over.1 = (bf16[512,2048]{1,0:T(8,128)(2,1)}, bf16[512,2048]{1,0:T(8,128)(2,1)}, f32[256,512]{1,0:T(8,128)}, f32[64,256]{1,0:T(8,128)}, f32[64,256]{1,0:T(8...) custom-call(bf16[512,2048]{1,0:T(8,128)(2,1)} %get-tuple-element.68.refs_0_, ...), custom_call_target="tpu_custom_call" | custom-call | tf_op jit(solution)/shard_map/hand_over/pallas_call | solution.py:1941
  322.6 1.3 fusion
  (1 shorter events, 0.0 us)
where the time goes:
time: 324 us
  Pallas kernels  320 us (99%)
    pallas_call x1, Pallas kernels, way_back(): pl.pallas_call(functools.partial(return_kernel, chain, places), out_shape...  122 us
    pallas_call x1, Pallas kernels, attend(): pl.pallas_call(functools.partial(attend_kernel, chain, places), out_shape...  106 us
    pallas_call x1, Pallas kernels, feed(): pl.pallas_call(functools.partial(feed_kernel, chain), out_shape=[shape(at...  84.4 us
    pallas_call x1, Pallas kernels, hand_over(): pl.pallas_call(functools.partial(hand_over_kernel, count), out_shape=[jax...  7.45 us

commit v1 on v0

--- a/solution.py
+++ b/solution.py
@@ -305,6 +305,7 @@
 
 MESH_ID = pl.DeviceIdType.MESH
 VMEM_BYTES = 63 * 2**20
+LEAD = 4
 
 
 def token_device(flip):
@@ -430,10 +431,12 @@
 class LineSum:
     FIRST, SECOND = 1, 3
 
-    def __init__(self, term, passing, total, sems, parts=1):
+    def __init__(self, term, passing, total, sems, parts=1, early=None, given=0):
         self.term, self.passing, self.total, self.sems = term, passing, total, sems
         self.parts, self.blocks = parts, term.shape[0]
         self.count = self.blocks * parts
+        self.early = self.count if early is None else early
+        self.given = given
         here, tokens = lax.axis_index("heads"), lax.axis_index("tokens")
         self.inner = (here == 1) | (here == 2)
         self.mate = (tokens, jnp.where(here < 2, 1 - here, 5 - here))
@@ -444,24 +447,26 @@
         start = multiple(quotient(i, self.blocks) * rows, rows) if self.parts > 1 else 0
         return remainder(i, self.blocks), pl.ds(start, rows)
 
-    def copy(self, src, dst, kind, i, device):
+    def copy(self, src, dst, send, recv, i, device):
         block, rows = self.place(i)
         return remote(
-            src.at[block, rows],
-            dst.at[block, rows],
-            self.sems.at[kind, i],
-            self.sems.at[kind + 1, i],
-            device,
+            src.at[block, rows], dst.at[block, rows], self.sems.at[send, i], self.sems.at[recv, i], device
         )
 
     def out_copy(self, i):
-        return self.copy(self.term, self.passing, 0, i, self.mate)
-
-    def across_copy(self, i):
-        return self.copy(self.passing, self.total, 2, i, self.across)
+        return self.copy(self.term, self.passing, 0, 1, i, self.mate)
+
+    def across_copy(self, i, src=None):
+        return self.copy(self.passing if src is None else src, self.total, 0, 2, i, self.across)
+
+    def start_given(self):
+        @pl.when(self.inner)
+        def _():
+            for i in range(self.given):
+                self.across_copy(i, self.term).start()
 
     def back_copy(self, i):
-        return self.copy(self.total, self.total, 4, i, self.mate)
+        return self.copy(self.total, self.total, 3, 1, i, self.mate)
 
     def add(self, out, other, i):
         block, rows = self.place(i)
@@ -488,14 +493,28 @@
             self.add(self.passing, self.term, i)
             self.across_copy(i).start()
 
-        def settle():
+        def settle(src):
             self.across_copy(j).wait_recv()
-            self.add(self.total, self.passing, j)
+            self.add(self.total, src, j)
             self.back_copy(j).start()
 
-        self.due(now, jnp.logical_not(self.inner), lambda: self.out_copy(now).start())
-        self.due(i, self.inner, pass_on)
-        self.due(j, self.inner, settle)
+        if self.early < self.count:
+            end = jnp.logical_not(self.inner) & (now >= self.early)
+            self.due(now, end, lambda: self.out_copy(now).start())
+        if self.given:
+            self.due(i, self.inner & (i >= self.given), pass_on)
+            self.due(j, self.inner & (j < self.given), lambda: settle(self.term))
+            self.due(j, self.inner & (j >= self.given), lambda: settle(self.passing))
+        else:
+            self.due(i, self.inner, pass_on)
+            self.due(j, self.inner, lambda: settle(self.passing))
+
+    def send(self, first, count):
+        @pl.when(jnp.logical_not(self.inner))
+        def _():
+            @pl.loop(0, count)
+            def _(i):
+                self.out_copy(first + i).start()
 
     def steps(self):
         return self.count + self.SECOND
@@ -521,7 +540,11 @@
             self.back_copy(i).wait_send()
 
         self.each(self.inner, sent)
-        self.each(jnp.logical_not(self.inner), lambda i: self.out_copy(i).wait_send())
+        @pl.when(jnp.logical_not(self.inner))
+        def _():
+            @pl.loop(self.given, self.count)
+            def _(i):
+                self.out_copy(i).wait_send()
 
 
 def quotient(a, b):
@@ -588,9 +611,9 @@
 
 
 def attend_kernel(
-    chain, places, x, small, key_shard, value_shard, inverse, query_shard, out_shard, gate_shard, up_shard,
+    chain, places, x, ids, gains, key_shard, value_shard, inverse, query_shard, out_shard, gate_shard, up_shard,
     down_shard, gate_full, up_full, down_full, query_full, pair_full, out_full, attn_sum, normed_out, query_out,
-    pairs, attended_out, log_out, cos_out, sin_out, small_out, gate_here, up_here, down_here, small_all, query_here, pair_here, pair_shard,
+    pairs, attended_out, log_out, cos_out, sin_out, small_out, small, gate_here, up_here, down_here, small_all, query_here, pair_here, pair_shard,
     out_here, pre_row, normed, query, attended, log_total, cos_table, sin_table, key_side, value_side, marks,
     scores, peak, mixed, near_pairs, term, passing, total, small_sems, gather_sems, local_sems, pair_sems,
     chain_sems, store_sems, load_sems,
@@ -609,6 +632,9 @@
     ]
     for load in loads:
         load.start()
+    small[...] = jnp.zeros(small.shape, jnp.float32)
+    small[0:1, :] = ids[...].astype(jnp.float32)
+    small[1:2, :] = gains[...]
     greet(range(1, 8), chain)
 
     def small_copy(flip):
@@ -865,6 +891,7 @@
 
     down.start()
     line = LineSum(term, passing, total, chain_sems, 2)
+    line.send(0, line.count)
     relays = [
         (at, at, 1, lambda _, job=job: job())
         for at, job in (
@@ -906,7 +933,7 @@
 
 
 def attend(
-    chain, places, x, small, key_weight, value_weight, inverse, query_weight, out_weight, gate_weight, up_weight,
+    chain, places, x, ids, gains, key_weight, value_weight, inverse, query_weight, out_weight, gate_weight, up_weight,
     down_weight,
 ):
     tokens, width = x.shape
@@ -915,6 +942,7 @@
     bf16, f32 = jnp.bfloat16, jnp.float32
     row = places * tokens
     each = width // (2 * count)
+    small = (8, tokens)
     anywhere, vmem = pl.BlockSpec(memory_space=pl.ANY), pl.BlockSpec(memory_space=pltpu.VMEM)
     shape = jax.ShapeDtypeStruct
     chunks = (2 * count, tokens, each)
@@ -933,18 +961,19 @@
         shape((tokens, 128), f32),
         shape((tokens, 128), f32),
         shape((tokens, 128), f32),
-        shape((8,) + small.shape, f32),
+        shape((8,) + small, f32),
     ]
     return pl.pallas_call(
         functools.partial(attend_kernel, chain, places),
         out_shape=out_shape,
-        in_specs=[vmem] * 5 + [anywhere] * 5,
+        in_specs=[vmem] * 6 + [anywhere] * 5,
         out_specs=[anywhere] * len(out_shape),
         scratch_shapes=[
+            pltpu.VMEM(small, f32),
             pltpu.VMEM(gate_weight.shape, bf16),
             pltpu.VMEM(up_weight.shape, bf16),
             pltpu.VMEM(down_weight.shape, bf16),
-            pltpu.VMEM((8,) + small.shape, f32),
+            pltpu.VMEM((8,) + small, f32),
             pltpu.VMEM((width, heads_wide), bf16),
             pltpu.VMEM((width, 128), bf16),
             pltpu.VMEM((width // 8, 128), bf16),
@@ -970,7 +999,7 @@
             pltpu.SemaphoreType.DMA((2, 7, Gather.COPIES)),
             pltpu.SemaphoreType.DMA((7,)),
             pltpu.SemaphoreType.DMA((2, 3)),
-            pltpu.SemaphoreType.DMA((6, 4 * count)),
+            pltpu.SemaphoreType.DMA((4, 4 * count)),
             pltpu.SemaphoreType.DMA((len(out_shape),)),
             pltpu.SemaphoreType.DMA((3,)),
         ],
@@ -979,7 +1008,7 @@
         ),
         name="attend_forward",
     )(
-        x, small, key_weight.T, value_weight.T, inverse, query_weight, out_weight, gate_weight, up_weight,
+        x, ids, gains, key_weight.T, value_weight.T, inverse, query_weight, out_weight, gate_weight, up_weight,
         down_weight,
     )
 
@@ -1068,10 +1097,16 @@
                 total = self.own[0, place].astype(jnp.float32)
                 for slot in slots:
                     total = total + self.near[slot, here].astype(jnp.float32)
-                out[place, :] = total
+                out[place, :] = total.astype(out.dtype)
 
         for slot in range(self.COPIES):
             self.copy(slot).wait_send()
+
+    def halfway(self):
+        for slot, (k, half) in enumerate(((0, 0), (2, 0), (0, 1), (1, 1))):
+            self.copy(slot).wait_recv()
+            self.copy(slot).wait_send()
+            self.add_near(k, half, slot)
 
 
 def block_order(i):
@@ -1090,8 +1125,9 @@
 
 def feed_kernel(
     chain, small_all, x_in, attn_in, cotangent_in, gate_full, up_full, down_full, back_sum, hidden_out, mlp_term,
-    scale_out, grad_gate_out, grad_up_out, x, attn_sum, cotangent, hidden, scale, grad_gate, grad_up, gate, up, down, mid_row, normed, back_gate, back_up, term, passing, total,
-    own_gate, near_gate, own_up, near_up, load_sems, swap_sems, chain_sems, reduce_sems, store_sems,
+    scale_out, grad_gate_out, up_out, x, attn_sum, cotangent, hidden, scale, grad_gate, gate, up, down, mid_row, normed, back_gate, back_up, term, passing, total,
+    own_gate, near_gate, own_up, near_up, mlp_near, load_sems, swap_sems, chain_sems, reduce_sems, store_sems,
+    lead_sems,
 ):
     count = term.shape[0] // 2
     each = term.shape[2]
@@ -1100,7 +1136,7 @@
     me = lax.axis_index("tokens")
     tiles = tiles_of(inner, 512)
     early = [
-        pltpu.make_async_copy(src, dst, load_sems.at[4, k])
+        pltpu.make_async_copy(src, dst, load_sems.at[k])
         for k, (src, dst) in enumerate(((x_in, x), (attn_in, attn_sum), (cotangent_in, cotangent)))
     ]
     loads = []
@@ -1108,9 +1144,9 @@
         cut = pl.ds(low, high - low)
         loads.append(
             (
-                pltpu.make_async_copy(gate_full.at[:, cut], gate.at[:, cut], load_sems.at[0, k]),
-                pltpu.make_async_copy(up_full.at[:, cut], up.at[:, cut], load_sems.at[1, k]),
-                pltpu.make_async_copy(down_full.at[cut, :], down.at[cut, :], load_sems.at[2, k]),
+                pltpu.make_async_copy(gate_full.at[:, cut], gate.at[:, cut], load_sems.at[4 + 3 * k]),
+                pltpu.make_async_copy(up_full.at[:, cut], up.at[:, cut], load_sems.at[5 + 3 * k]),
+                pltpu.make_async_copy(down_full.at[cut, :], down.at[cut, :], load_sems.at[6 + 3 * k]),
             )
         )
     for load in early:
@@ -1150,9 +1186,11 @@
                 )
         return found
 
-    def mid_pair(n, row, rows):
+    ahead = 3
+
+    def mid_pair(n, row):
         cut = pl.ds(pl.multiple_of(n * 2 * each, 2 * each), 2 * each)
-        place = pl.ds(row, rows)
+        place = pl.ds(row, half)
         made = nt_dot(back_gate[place, :], gate[cut, :]) + nt_dot(back_up[place, :], up[cut, :])
         made = made.astype(jnp.bfloat16)
         term[2 * n, place] = made[:, :each]
@@ -1209,9 +1247,10 @@
 
         @pl.when(part == 0)
         def _():
-            @pl.loop(0, count)
+            @pl.loop(0, ahead)
             def _(n):
-                mid_pair(n, 0, half)
+                mid_pair(n, 0)
+                line.send(2 * n, 2)
 
     stores = []
 
@@ -1224,27 +1263,41 @@
     store(scale, scale_out)
 
     def mlp_place(n):
-        rows = pl.ds(pl.multiple_of(lax.rem(n, 4) * tokens, tokens), tokens)
-        return rows, lax.div(n, 4) * 2 * each
-
-    def mlp_stores(n):
-        rows, low = mlp_place(n)
-        return [
-            pltpu.make_async_copy(
-                gate.at[rows, pl.ds(pl.multiple_of(low + k * each, each), each)],
-                mlp_term.at[2 * n + k],
-                load_sems.at[3, 2 * n + k],
-            )
-            for k in range(2)
-        ]
+        rows = pl.ds(multiple(remainder(n, 4) * tokens, tokens), tokens)
+        return rows, quotient(n, 4) * 2 * each
+
+    def mlp_at(c):
+        rows, low = mlp_place(quotient(c, 2))
+        low = low + remainder(c, 2) * each
+        return gate.at[rows, pl.ds(multiple(low, each), each)]
+
+    lead = mlp_near.shape[0]
+
+    def lead_copy(c):
+        return remote(
+            mlp_at(c), mlp_near.at[c], lead_sems.at[0, c], lead_sems.at[1, c], line.mate
+        )
 
     def mlp_pair(n):
         cut = pl.ds(pl.multiple_of(n * 2 * each, 2 * each), 2 * each)
         made = jnp.dot(hidden[...], down[:, cut], preferred_element_type=jnp.float32)
         rows, low = mlp_place(n)
         gate[rows, pl.ds(pl.multiple_of(low, 2 * each), 2 * each)] = made.astype(jnp.bfloat16)
-        for copy in mlp_stores(n):
-            copy.start()
+
+        @pl.when(n >= lead // 2)
+        def _():
+            for k in range(2):
+                pltpu.make_async_copy(
+                    mlp_at(2 * n + k), mlp_term.at[2 * n + k], load_sems.at[3]
+                ).start()
+
+        @pl.when((n < lead // 2) & jnp.logical_not(line.inner))
+        def _():
+            for k in range(2):
+                lead_copy(2 * n + k).start()
+
+    def lead_store(c):
+        return pltpu.make_async_copy(mlp_near.at[c], mlp_term.at[c], lead_sems.at[2, c])
 
     gate_sum = Reduce(own_gate, near_gate, reduce_sems.at[0])
     up_sum = Reduce(own_up, near_up, reduce_sems.at[1])
@@ -1259,39 +1312,74 @@
             for copy in swaps_of(part)[which]:
                 copy.wait_recv()
 
+    def late_pair(i):
+        i = i + ahead
+        part = jnp.where(i < count, 0, 1)
+        n = i - part * count
+        mid_pair(n, pl.multiple_of(part * half, half))
+        line.send(part * 2 * count + 2 * n, 2)
+
+    def late_pairs(i):
+        late_pair(2 * i)
+
+        @pl.when(2 * i + 1 + ahead < 2 * count)
+        def _():
+            late_pair(2 * i + 1)
+
     begun = 2 * len(tiles)
+    last_pairs = (2 * count - ahead + 1) // 2 - 1
     plan = (
-        (begun, begun, 1, lambda _: received(slice(0, 1))),
-        (begun, begun, 1, lambda _: received(slice(1, None, 2))),
-        (begun, begun + 3, 1, lambda i: grad_block(gate_sum, back_gate, block_order(i))),
-        (begun, begun + count - 1, 1, lambda i: mid_pair(i, half, half)),
-        (begun + 4, begun + 4, 1, lambda _: received(slice(2, None, 2))),
-        (begun + 4, begun + 7, 1, lambda i: grad_block(up_sum, back_up, block_order(i))),
-        (begun + 8, begun + 8, 1, lambda _: gate_sum.second()),
-        (begun + 9, begun + 2 * count + 7, 2, mlp_pair),
-        (begun + 16, begun + 16, 1, lambda _: up_sum.second()),
-    )
-
-    @pl.loop(begun, line.steps())
+        (0, last_pairs, 1, late_pairs),
+        (0, 0, 1, lambda _: received(slice(0, 1))),
+        (0, 0, 1, lambda _: received(slice(1, None, 2))),
+        (0, 3, 1, lambda i: grad_block(gate_sum, back_gate, block_order(i))),
+        (4, 4, 1, lambda _: received(slice(2, None, 2))),
+        (4, 7, 1, lambda i: grad_block(up_sum, back_up, block_order(i))),
+        (7, 7, 1, lambda _: gate_sum.second()),
+        (last_pairs + 1, last_pairs + count, 1, mlp_pair),
+    )
+
+    @pl.loop(0, (line.steps() - begun + 1) // 2)
     def _(now):
         by_step(now, plan)
-        line.step(now)
+        line.step(begun + 2 * now)
+        line.step(begun + 2 * now + 1)
 
     gate_sum.finish(grad_gate)
     store(grad_gate, grad_gate_out)
     line.receive_all()
     store(total, back_sum)
-    up_sum.finish(grad_up)
-    store(grad_up, grad_up_out)
+    @pl.when(line.inner)
+    def _():
+        for c in range(lead):
+            lead_copy(c).wait_recv()
+            mlp_near[c] = (
+                mlp_near[c].astype(jnp.float32) + mlp_at(c)[...].astype(jnp.float32)
+            ).astype(mlp_near.dtype)
+            lead_store(c).start()
+
+    up_sum.halfway()
+    rows = span // 2
+    store(own_up.at[0], up_out.at[pl.ds(0, span), :])
+    store(own_up.at[2, pl.ds(0, rows)], up_out.at[pl.ds(span, rows), :])
+    store(own_up.at[1, pl.ds(rows, rows)], up_out.at[pl.ds(span + rows, rows), :])
     line.finish()
     for part in range(2):
         for copy in swaps_of(part):
             copy.wait_send()
 
-    @pl.loop(0, count)
-    def _(n):
-        for copy in mlp_stores(n):
-            copy.wait()
+    rest = pl.ds(lead, 2 * count - lead)
+    pltpu.make_async_copy(term.at[rest], total.at[rest], load_sems.at[3]).wait()
+
+    @pl.when(line.inner)
+    def _():
+        for c in range(lead):
+            lead_store(c).wait()
+
+    @pl.when(jnp.logical_not(line.inner))
+    def _():
+        for c in range(lead):
+            lead_copy(c).wait_send()
 
     for copy in stores:
         copy.wait()
@@ -1313,8 +1401,8 @@
             shape((tokens, inner), bf16),
             shape(attn_sum.shape, bf16),
             shape((tokens, 128), f32),
-            shape((span, inner), f32),
-            shape((span, inner), f32),
+            shape((span, inner), bf16),
+            shape((2 * span, inner), bf16),
         ],
         in_specs=[vmem] + [anywhere] * 6,
         out_specs=[anywhere] * 6,
@@ -1324,8 +1412,7 @@
             pltpu.VMEM((tokens, width), bf16),
             pltpu.VMEM((tokens, inner), bf16),
             pltpu.VMEM((tokens, 128), f32),
-            pltpu.VMEM((span, inner), f32),
-            pltpu.VMEM((span, inner), f32),
+            pltpu.VMEM((span, inner), bf16),
             pltpu.VMEM((width, inner), bf16),
             pltpu.VMEM((width, inner), bf16),
             pltpu.VMEM((inner, width), bf16),
@@ -1340,11 +1427,13 @@
             pltpu.VMEM((6, span // 2, inner), bf16),
             pltpu.VMEM((4, span, inner), bf16),
             pltpu.VMEM((6, span // 2, inner), bf16),
-            pltpu.SemaphoreType.DMA((5, max(tiles, 2 * count))),
+            pltpu.VMEM((LEAD, tokens, 128), bf16),
+            pltpu.SemaphoreType.DMA((4 + 3 * tiles,)),
             pltpu.SemaphoreType.DMA((2, 2 + 4 * tiles)),
-            pltpu.SemaphoreType.DMA((6, 4 * count)),
+            pltpu.SemaphoreType.DMA((4, 4 * count)),
             pltpu.SemaphoreType.DMA((2, 2, Reduce.COPIES)),
-            pltpu.SemaphoreType.DMA((5,)),
+            pltpu.SemaphoreType.DMA((8,)),
+            pltpu.SemaphoreType.DMA((3, LEAD)),
         ],
         compiler_params=pltpu.CompilerParams(
             collective_id=1, has_side_effects=True, vmem_limit_bytes=VMEM_BYTES
@@ -1363,12 +1452,12 @@
 
 def return_kernel(
     chain, places, small_all, query, pairs, log_total, cos_table, sin_table, scale,
-    attended_in, x_in, attn_in, back_sum, query_full, pair_full, out_full, mlp_term, hidden_in, cotangent, normed_in, layer_out, grad_input, grad_down_out,
-    grad_query, grad_key, grad_value, grad_out_out, gains, mid_part, grad_down, grad_out, pair_back, grad_in, in_here, out_here, key_side, value_side, query_side, back_side, back_att,
+    attended_in, x_in, attn_in, back_sum, query_full, pair_full, out_full, mlp_term, hidden_in, cotangent, normed_in, up_in, layer_out, grad_input, grad_down_out,
+    grad_query, grad_key, grad_value, grad_out_out, grad_up_out, gains, mid_part, grad_down, grad_out, pair_back, grad_in, in_here, out_here, key_side, value_side, query_side, back_side, back_att,
     back_rows, back_keys, back_values, pair_out, pair_near, normed, back_attn, hidden, cotangents, att_low,
     back_all, pre_row, pre_part, gains_near, mlp_sum, mlp_passing, mlp_total, term, passing, total, own_down,
-    near_down, own_in, near_in, own_out, near_out, load_sems, swap_sems, pair_sems, gain_sems, chain_sems,
-    reduce_sems, store_sems,
+    near_down, own_in, near_in, own_out, near_out, load_sems, swap_sems, pair_sems, gain_sems, mlp_sems, chain_sems,
+    reduce_sems, store_sems, up_half, up_near, up_sems,
 ):
     count = term.shape[0] // 2
     each = term.shape[2]
@@ -1399,18 +1488,18 @@
         low = multiple(remainder(c, 2) * each, each)
         return own_down.at[quotient(c, 4), pl.ds(row, tokens), pl.ds(low, each)]
 
-    loads = []
     for c in range(2 * count):
         side = key_side if c < count else value_side
-        loads.append(load(16 + c, back_sum.at[c], back_at(side, c % count)))
-        loads.append(load(16 + 2 * count + c, x_in.at[:, pl.ds(c * each, each)], term.at[c]))
-        loads.append(load(16 + 4 * count + c, attn_in.at[c], attn_at(c)))
+        load(9, back_sum.at[c], back_at(side, c % count))
+        load(10, x_in.at[:, pl.ds(c * each, each)], term.at[c])
+        load(11, attn_in.at[c], attn_at(c))
     load_out = load(0, out_full, out_here)
     heads_wide = query.shape[1]
     load_in = load(1, query_full, in_here.at[:, pl.ds(0, heads_wide)])
     load_pair = load(6, pair_full, in_here.at[:, pl.ds(heads_wide, 128)])
     load_hidden = load(3, hidden_in, hidden.at[mine, :])
     load_normed = load(4, normed_in, normed.at[mine, :])
+    load_up = load(13, up_in, up_half)
     greet(range(1, 8), chain)
 
     def swap(k, ref):
@@ -1434,15 +1523,27 @@
             token_device(flip),
         )
 
-    mlp_line = LineSum(mlp_sum, mlp_passing, mlp_total, chain_sems.at[0])
+    mlp_line = LineSum(mlp_sum, mlp_passing, mlp_total, mlp_sems, given=LEAD)
     load_mlp.wait()
-    mlp_line.step(0)
+    mlp_line.start_given()
+    mlp_line.send(LEAD, 2 * count - LEAD)
+    rows_up = up_near.shape[1]
+
+    def up_copy(slot):
+        return remote(
+            up_half.at[pl.ds((2 + slot) * rows_up, rows_up), :],
+            up_near.at[slot],
+            up_sems.at[0, slot],
+            up_sems.at[1, slot],
+            token_device((4, 2)[slot]),
+        )
+
     for k in range(8):
         pre_row[:, k * span : (k + 1) * span] = jnp.broadcast_to(
             small_all[k, 1:2, span : 2 * span], (8, span)
         )
-    for copy in loads:
-        copy.wait()
+    for k in (9, 10, 11):
+        pltpu.make_async_copy(attn_in, term, load_sems.at[k]).wait()
     load_cot.wait()
 
     def hat_at(c):
@@ -1466,7 +1567,11 @@
     summed_here[...] = jnp.broadcast_to(mean, summed_here.shape)
     for flip in range(1, 8):
         gain_copy(1, mid_part, flip).start()
-    mlp_line.step(1)
+    mlp_line.step(LineSum.SECOND)
+    load_up.wait()
+    for slot in range(2):
+        up_copy(slot).start()
+
     for base, side in ((0, key_side), (count, value_side)):
 
         @pl.loop(0, count)
@@ -1478,7 +1583,7 @@
                 jnp.bfloat16
             )
 
-    mlp_line.step(2)
+    mlp_line.step(LineSum.SECOND + 1)
     load_attended.wait()
     att_low[mine, :] = attended[...].astype(jnp.bfloat16)
     swap_back = swap(0, back_attn)
@@ -1505,7 +1610,7 @@
     load_out.wait()
     back_att[...] = nt_dot(back_attn[mine, :], out_here[...]).astype(jnp.bfloat16)
     swap_cot = swap(2, cotangents)
-    mlp_line.step(3)
+    mlp_line.step(LineSum.SECOND + 2)
     load_hidden.wait()
     swap_hidden = swap(3, hidden)
 
@@ -1532,7 +1637,7 @@
     load_in.wait()
     load_pair.wait()
 
-    begun = 4
+    begun = LineSum.SECOND + 3
     back_rows[...] = jnp.zeros_like(back_rows)
 
     def key_step(k, diagonal):
@@ -1628,6 +1733,7 @@
         made = nt_dot(back_all[mine, :], in_here[cut, :]).astype(jnp.bfloat16)
         term[2 * n] = made[:, :each]
         term[2 * n + 1] = made[:, each:]
+        line.send(2 * n, 2)
 
     def cut_of(k):
         index = jnp.bitwise_xor(me, 2 * k)
@@ -1653,22 +1759,15 @@
         k = block_order(i)
         out_sum.put(k, tn_dot(att_low[...], back_attn[:, cut_of(k)]))
 
-    def late_loads():
-        copies = [pltpu.make_async_copy(x_in, cotangents.at[theirs, :], load_sems.at[8])]
-        for c in range(2 * count):
-            copies.append(
-                pltpu.make_async_copy(
-                    attn_in.at[c],
-                    cotangents.at[mine, pl.ds(c * each, each)],
-                    load_sems.at[16 + c],
-                )
-            )
-        return copies
-
     def load_late():
         swap_cot.wait_send()
-        for copy in late_loads():
-            copy.start()
+        load(8, x_in, cotangents.at[theirs, :])
+        for c in range(2 * count):
+            load(12, attn_in.at[c], cotangents.at[mine, pl.ds(c * each, each)])
+
+    def wait_late():
+        for k in (8, 12):
+            pltpu.make_async_copy(x_in, cotangents.at[mine, :], load_sems.at[k]).wait()
 
     def x_at(c):
         return cotangents[theirs, cut_at(c)].astype(jnp.float32)
@@ -1682,13 +1781,14 @@
         (grad_in.at[:, pl.ds(0, heads_wide)], grad_query),
         (pair_back.at[pl.ds(0, 64)], grad_key),
         (pair_back.at[pl.ds(64, 64)], grad_value),
+        (up_half.at[pl.ds(0, 2 * rows_up), :], grad_up_out),
     )
 
     def whole(k):
-        return pltpu.make_async_copy(*wholes[k], store_sems.at[4 * count + k])
-
-    def store_block(c, src, out, first):
-        return pltpu.make_async_copy(src.at[c], out.at[:, cut_at(c)], store_sems.at[first + c])
+        return pltpu.make_async_copy(*wholes[k], store_sems.at[2 + k])
+
+    def store_block(c, src, out, sem):
+        return pltpu.make_async_copy(src.at[c], out.at[:, cut_at(c)], store_sems.at[sem])
 
     def finish_mlp(_):
         mlp_line.receive_all()
@@ -1703,8 +1803,7 @@
     scale_here = back_keys.at[0]
 
     def scale_rows(_):
-        for copy in late_loads():
-            copy.wait()
+        wait_late()
         for k in range(8):
             pre_row[:, k * span : (k + 1) * span] = jnp.broadcast_to(
                 small_all[k, 1:2, :span], (8, span)
@@ -1735,9 +1834,23 @@
 
     def finish_in(_):
         in_sum.finish(grad_in)
-        pair_back[...] = grad_in[:, heads_wide:].T
+        pair_back[...] = grad_in[:, heads_wide:].astype(jnp.float32).T
         for k in (2, 3, 4):
             whole(k).start()
+
+    def finish_up(_):
+        for slot in range(2):
+            up_copy(slot).wait()
+
+            @pl.loop(0, rows_up // 32)
+            def _(i):
+                here = pl.ds(pl.multiple_of(i * 32, 32), 32)
+                place = pl.ds(pl.multiple_of(slot * rows_up + i * 32, 32), 32)
+                up_half[place, :] = (
+                    up_half[place, :].astype(jnp.float32) + up_near[slot, here].astype(jnp.float32)
+                ).astype(up_half.dtype)
+
+        whole(5).start()
 
     def finish_down(_):
         down_sum.finish(grad_down)
@@ -1747,7 +1860,7 @@
         out_sum.finish(grad_out)
         whole(1).start()
 
-    line = LineSum(term, passing, total, chain_sems.at[1], 2)
+    line = LineSum(term, passing, total, chain_sems, 2, 2 * count)
     steps = line.steps()
     behind = 14
 
@@ -1772,6 +1885,7 @@
         (20, 20, 1, finish_mlp),
         (21, 21, 1, lambda _: out_sum.second()),
         (23, 23, 1, lambda _: in_sum.second()),
+        (26, 26, 1, finish_up),
         (28, 28, 1, finish_down),
         (30, 30, 1, finish_out),
         (32, 32, 1, finish_in),
@@ -1807,7 +1921,7 @@
         u = total[c].astype(jnp.float32) * pre_row[0:1, cut]
         found = scale_here[...] * (u - x_at(c) * scale_here[...] * weighed[...])
         term[c] = (back_attn[mine, cut].astype(jnp.float32) + found).astype(jnp.bfloat16)
-        store_block(c, term, grad_input, 2 * count).start()
+        store_block(c, term, grad_input, 1).start()
 
     own = pl.ds(pl.multiple_of(me * span, span), span)
     gains_near[me, :, :span] = pre_part[:, own]
@@ -1829,15 +1943,13 @@
     for k in range(len(wholes)):
         whole(k).wait()
 
-    @pl.loop(0, 2 * count)
-    def _(c):
-        store_block(c, mlp_sum, layer_out, 0).wait()
-        store_block(c, term, grad_input, 2 * count).wait()
+    for k in range(2):
+        pltpu.make_async_copy(mlp_sum, term, store_sems.at[k]).wait()
 
 
 def way_back(
     chain, places, small_all, query, pairs, log_total, cos_table, sin_table, scale, attended, x, attn_sum, back_sum,
-    query_full, pair_full, out_full, mlp_term, hidden, cotangent, normed,
+    query_full, pair_full, out_full, mlp_term, hidden, cotangent, normed, up_half,
 ):
     tokens, width = x.shape
     inner = hidden.shape[1]
@@ -1855,21 +1967,22 @@
         out_shape=[
             shape((tokens, width), bf16),
             shape((tokens, width), bf16),
-            shape((inner, span), f32),
-            shape((span, heads_wide), f32),
+            shape((inner, span), bf16),
+            shape((span, heads_wide), bf16),
             shape((64, span), f32),
             shape((64, span), f32),
-            shape((heads_wide, span), f32),
+            shape((heads_wide, span), bf16),
+            shape((span, inner), bf16),
             shape((8, 2 * span), f32),
         ],
-        in_specs=[vmem] * 7 + [anywhere] * 11,
-        out_specs=[anywhere] * 7 + [vmem],
+        in_specs=[vmem] * 7 + [anywhere] * 12,
+        out_specs=[anywhere] * 8 + [vmem],
         scratch_shapes=[
             pltpu.VMEM((8, width), f32),
-            pltpu.VMEM((inner, span), f32),
-            pltpu.VMEM((heads_wide, span), f32),
+            pltpu.VMEM((inner, span), bf16),
+            pltpu.VMEM((heads_wide, span), bf16),
             pltpu.VMEM((128, span), f32),
-            pltpu.VMEM((span, wide), f32),
+            pltpu.VMEM((span, wide), bf16),
             pltpu.VMEM((width, wide), bf16),
             pltpu.VMEM((heads_wide, width), bf16),
             pltpu.VMEM((2, row, 128), bf16),
@@ -1903,13 +2016,17 @@
             pltpu.VMEM((6, span // 2, wide), bf16),
             pltpu.VMEM((4, heads_wide, span), bf16),
             pltpu.VMEM((6, heads_wide // 2, span), bf16),
-            pltpu.SemaphoreType.DMA((16 + 6 * count,)),
+            pltpu.SemaphoreType.DMA((14,)),
             pltpu.SemaphoreType.DMA((2, 6)),
             pltpu.SemaphoreType.DMA((2, places)),
             pltpu.SemaphoreType.DMA((2, 2, 7)),
-            pltpu.SemaphoreType.DMA((2, 6, 4 * count)),
+            pltpu.SemaphoreType.DMA((4, 2 * count)),
+            pltpu.SemaphoreType.DMA((4, 4 * count)),
             pltpu.SemaphoreType.DMA((3, 2, Reduce.COPIES)),
-            pltpu.SemaphoreType.DMA((4 * count + 5,)),
+            pltpu.SemaphoreType.DMA((8,)),
+            pltpu.VMEM((2 * span, inner), bf16),
+            pltpu.VMEM((2, span // 2, inner), bf16),
+            pltpu.SemaphoreType.DMA((2, 2)),
         ],
         compiler_params=pltpu.CompilerParams(
             collective_id=2, has_side_effects=True, vmem_limit_bytes=VMEM_BYTES
@@ -1917,37 +2034,60 @@
         name="way_back",
     )(
         small_all, query, pairs, log_total, cos_table, sin_table, scale, attended, x, attn_sum, back_sum,
-        query_full, pair_full, out_full, mlp_term, hidden, cotangent, normed,
-    )
-
-
-def hand_over_kernel(count, *refs):
-    ins, outs, held = refs[:count], refs[count : 2 * count], refs[2 * count : 3 * count]
-    sems = refs[3 * count]
+        query_full, pair_full, out_full, mlp_term, hidden, cotangent, normed, up_half,
+    )
+
+
+def hand_over_kernel(count, gains, *refs):
+    ins, outs = refs[:count], refs[count : 2 * count]
+    grad_pre, grad_mid = refs[2 * count : 2 * count + 2]
+    held, wide, sems = refs[2 * count + 2 : 3 * count + 2], refs[3 * count + 2 : -1], refs[-1]
     loads = [pltpu.make_async_copy(ins[k], held[k], sems.at[0, k]) for k in range(count)]
-    stores = [pltpu.make_async_copy(held[k], outs[k], sems.at[1, k]) for k in range(count)]
     for load in loads:
         load.start()
-    for load, store in zip(loads, stores):
+    span = gains.shape[1] // 2
+    grad_pre[...] = gains[0:1, :span]
+    grad_mid[...] = gains[0:1, span:]
+    stores = []
+    wide = list(wide)
+    for k, load in enumerate(loads):
         load.wait()
-        store.start()
+        ready = held[k]
+        if outs[k].dtype != ready.dtype:
+            ready = wide.pop(0)
+
+            @pl.loop(0, ready.shape[0] // 32)
+            def _(i):
+                here = pl.ds(pl.multiple_of(i * 32, 32), 32)
+                ready[here, :] = held[k][here, :].astype(ready.dtype)
+
+        stores.append(pltpu.make_async_copy(ready, outs[k], sems.at[1, k]))
+        stores[-1].start()
     for store in stores:
         store.wait()
 
 
-def hand_over(*arrays):
+def hand_over(gains, *arrays):
     count = len(arrays)
-    anywhere = pl.BlockSpec(memory_space=pl.ANY)
+    anywhere, vmem = pl.BlockSpec(memory_space=pl.ANY), pl.BlockSpec(memory_space=pltpu.VMEM)
+    half = jax.ShapeDtypeStruct((1, gains.shape[1] // 2), gains.dtype)
+    types = [array.dtype if k < 2 else jnp.dtype(jnp.float32) for k, array in enumerate(arrays)]
     return pl.pallas_call(
         functools.partial(hand_over_kernel, count),
-        out_shape=[jax.ShapeDtypeStruct(array.shape, array.dtype) for array in arrays],
-        in_specs=[anywhere] * count,
-        out_specs=[anywhere] * count,
+        out_shape=[jax.ShapeDtypeStruct(array.shape, kind) for array, kind in zip(arrays, types)]
+        + [half, half],
+        in_specs=[vmem] + [anywhere] * count,
+        out_specs=[anywhere] * count + [vmem, vmem],
         scratch_shapes=[pltpu.VMEM(array.shape, array.dtype) for array in arrays]
+        + [
+            pltpu.VMEM(array.shape, kind)
+            for array, kind in zip(arrays, types)
+            if kind != array.dtype
+        ]
         + [pltpu.SemaphoreType.DMA((2, count))],
         compiler_params=pltpu.CompilerParams(vmem_limit_bytes=VMEM_BYTES),
         name="hand_over",
-    )(*arrays)
+    )(gains, *arrays)
 
 
 def shards_cube(
@@ -1970,14 +2110,7 @@
     query_width = query_weight.shape[1]
     heads_here = query_width // head_size
     places = ROW // row_count
-    half = row_count // 2
-    gains = jnp.pad(pre_gain.astype(jnp.float32), (0, half)) + jnp.pad(
-        mid_gain.astype(jnp.float32), (half, 0)
-    )
-    sublane = lax.broadcasted_iota(jnp.int32, (8, row_count), 0)
-    small = jnp.where(
-        sublane == 0, segments.astype(jnp.float32)[None], jnp.where(sublane == 1, gains[None], 0.0)
-    )
+    gains = jnp.concatenate([pre_gain, mid_gain]).astype(jnp.float32)[None]
     half_size = head_size // 2
     inverse = 10000.0 ** (-np.arange(half_size, dtype=np.float32) / half_size)
     inverse = jnp.asarray(np.tile(inverse.astype(np.float32), (8, 128 // half_size)))
@@ -2001,7 +2134,8 @@
         chain,
         places,
         inputs,
-        small,
+        segments[None],
+        gains,
         key_weight,
         value_weight,
         inverse,
@@ -2011,10 +2145,10 @@
         up_weight,
         down_weight,
     )
-    back_sum, hidden, mlp_term, scale, grad_gate, grad_up = feed(
+    back_sum, hidden, mlp_term, scale, grad_gate, up_half = feed(
         chain, small_full, inputs, attn_sum, cotangent, gate_full, up_full, down_full
     )
-    layer_out, grad_input, grad_down, grad_query, grad_key, grad_value, grad_out, gains = way_back(
+    layer_out, grad_input, grad_down, grad_query, grad_key, grad_value, grad_out, grad_up, gains = way_back(
         chain,
         places,
         small_full,
@@ -2035,11 +2169,33 @@
         hidden,
         cotangent,
         normed,
-    )
-    grad_pre, grad_mid = jnp.split(gains[0], 2)
-    layer_out, grad_input, grad_query, grad_key, grad_value, grad_out, grad_gate, grad_up, grad_down = hand_over(
-        layer_out, grad_input, grad_query, grad_key, grad_value, grad_out, grad_gate, grad_up, grad_down
-    )
+        up_half,
+    )
+    (
+        layer_out,
+        grad_input,
+        grad_query,
+        grad_key,
+        grad_value,
+        grad_out,
+        grad_gate,
+        grad_up,
+        grad_down,
+        grad_pre,
+        grad_mid,
+    ) = hand_over(
+        gains,
+        layer_out,
+        grad_input,
+        grad_query,
+        grad_key,
+        grad_value,
+        grad_out,
+        grad_gate,
+        grad_up,
+        grad_down,
+    )
+    grad_pre, grad_mid = grad_pre[0], grad_mid[0]
     grad_key, grad_value = grad_key.T, grad_value.T
     return (
         layer_out,

time: 324 us -> 306 us (0.944)
  Pallas kernels: 320 us -> 303 us
    pallas_call x1, Pallas kernels: 122 us -> 114 us  [way_back(): pl.pallas_call(functools.partial(return_kernel, chain, places), out_shape...]
    pallas_call x1, Pallas kernels: 84.4 us -> 77.2 us  [feed(): pl.pallas_call(functools.partial(feed_kernel, chain), out_shape=[shape(at...]
where the time goes in v1:
time: 306 us
  Pallas kernels  303 us (99%)
    pallas_call x1, Pallas kernels, way_back(): pl.pallas_call(functools.partial(return_kernel, chain, places), out_shape...  114 us
    pallas_call x1, Pallas kernels, attend(): pl.pallas_call(functools.partial(attend_kernel, chain, places), out_shape...  105 us
    pallas_call x1, Pallas kernels, feed(): pl.pallas_call(functools.partial(feed_kernel, chain), out_shape=[shape(at...  77.2 us
    pallas_call x1, Pallas kernels, hand_over(): pl.pallas_call(functools.partial(hand_over_kernel, count), out_shape=[jax...  6.99 us

profile of v1, /device:TPU:0, one launch (start us, length us, event | category | flops | bytes accessed | tf_op | source)
XLA Modules:
  0.0 305.5 jit_solution(14412534836370880197)
XLA Ops:
  0.6 0.7 concatenate.14
  1.3 0.7 concatenate.15
  2.0 0.6 maximum_convert_fusion.gains
  2.5 104.5 %attend_forward.1 = (bf16[2048,1408]{1,0:T(8,128)(2,1)}, bf16[2048,1408]{1,0:T(8,128)(2,1)}, bf16[1408,2048]{1,0:T(8,128)(2,1)}, bf16[2048,512]{1,0:T(8,128)(2,1...) custom-call(bf16[512,2048]{1,0:T(8,128)(2,1)} %x_in.3, ...), custom_call_target="tpu_custom_call" | custom-call | tf_op jit(solution)/shard_map/attend_forward/pallas_call | solution.py:966
  107.1 77.2 %feed_forward.1 = (bf16[16,512,128]{2,1,0:T(8,128)(2,1)}, bf16[512,1408]{1,0:T(8,128)(2,1)}, bf16[16,512,128]{2,1,0:T(8,128)(2,1)}, f32[512,128]{1,0:T(8,128)}, ...) custom-call(f32[8,8,512]{2,1,0:T(8,128)} %get-tuple-element.52.small_all, bf16[512,2048]{1,0:T(8,128)(2,1)} %x_in.3, ...), custom_call_target="tpu_custom_call" | custom-call | tf_op jit(solution)/shard_map/feed_forward/pallas_call | solution.py:1397
  184.3 114.1 %way_back.1 = (bf16[512,2048]{1,0:T(8,128)(2,1)}, bf16[512,2048]{1,0:T(8,128)(2,1)}, bf16[1408,256]{1,0:T(8,128)(2,1)}, bf16[256,512]{1,0:T(8,128)(2,1)}, f32[64...) custom-call(f32[8,8,512]{2,1,0:T(8,128)} %get-tuple-element.52.small, ...), custom_call_target="tpu_custom_call" | custom-call | tf_op jit(solution)/shard_map/way_back/pallas_call | solution.py:1965
  298.4 7.0 %hand_over.1 = (bf16[512,2048]{1,0:T(8,128)(2,1)}, bf16[512,2048]{1,0:T(8,128)(2,1)}, f32[256,512]{1,0:T(8,128)}, f32[64,256]{1,0:T(8,128)}, f32[64,256]{1,0:T(8...) custom-call(f32[8,512]{1,0:T(8,128)} %get-tuple-element.72.gains, ...), custom_call_target="tpu_custom_call" | custom-call | tf_op jit(solution)/shard_map/hand_over/pallas_call | solution.py:2075

commit v2 on v1

--- a/solution.py
+++ b/solution.py
@@ -305,7 +305,7 @@
 
 MESH_ID = pl.DeviceIdType.MESH
 VMEM_BYTES = 63 * 2**20
-LEAD = 4
+LEAD = 2
 
 
 def token_device(flip):
@@ -429,14 +429,15 @@
 
 
 class LineSum:
-    FIRST, SECOND = 1, 3
-
-    def __init__(self, term, passing, total, sems, parts=1, early=None, given=0):
+    FIRST = 1
+
+    def __init__(self, term, passing, total, sems, parts=1, early=None, given=0, second=5):
         self.term, self.passing, self.total, self.sems = term, passing, total, sems
         self.parts, self.blocks = parts, term.shape[0]
         self.count = self.blocks * parts
         self.early = self.count if early is None else early
         self.given = given
+        self.second = second
         here, tokens = lax.axis_index("heads"), lax.axis_index("tokens")
         self.inner = (here == 1) | (here == 2)
         self.mate = (tokens, jnp.where(here < 2, 1 - here, 5 - here))
@@ -470,9 +471,7 @@
 
     def add(self, out, other, i):
         block, rows = self.place(i)
-        out[block, rows] = (
-            out[block, rows].astype(jnp.float32) + other[block, rows].astype(jnp.float32)
-        ).astype(out.dtype)
+        out[block, rows] = out[block, rows] + other[block, rows]
 
     def due(self, i, who, job):
         if isinstance(i, int):
@@ -486,7 +485,7 @@
             job()
 
     def step(self, now):
-        i, j = now - self.FIRST, now - self.SECOND
+        i, j = now - self.FIRST, now - self.second
 
         def pass_on():
             self.out_copy(i).wait_recv()
@@ -502,9 +501,9 @@
             end = jnp.logical_not(self.inner) & (now >= self.early)
             self.due(now, end, lambda: self.out_copy(now).start())
         if self.given:
-            self.due(i, self.inner & (i >= self.given), pass_on)
             self.due(j, self.inner & (j < self.given), lambda: settle(self.term))
             self.due(j, self.inner & (j >= self.given), lambda: settle(self.passing))
+            self.due(i, self.inner & (i >= self.given), pass_on)
         else:
             self.due(i, self.inner, pass_on)
             self.due(j, self.inner, lambda: settle(self.passing))
@@ -517,7 +516,7 @@
                 self.out_copy(first + i).start()
 
     def steps(self):
-        return self.count + self.SECOND
+        return self.count + self.second
 
     def each(self, who, job):
         @pl.when(who)
@@ -534,17 +533,32 @@
     def receive_all(self):
         self.each(jnp.logical_not(self.inner), lambda i: self.back_copy(i).wait_recv())
 
-    def finish(self):
-        def sent(i):
-            self.across_copy(i).wait_send()
-            self.back_copy(i).wait_send()
-
-        self.each(self.inner, sent)
+    def collect(self, out, sem):
+        @pl.loop(0, self.count)
+        def _(i):
+            self.receive(i)
+            block, rows = self.place(i)
+            pltpu.make_async_copy(self.total.at[block, rows], out.at[block, rows], sem).start()
+
+        return pltpu.make_async_copy(self.total, out, sem)
+
+    def finish_ends(self):
         @pl.when(jnp.logical_not(self.inner))
         def _():
             @pl.loop(self.given, self.count)
             def _(i):
                 self.out_copy(i).wait_send()
+
+    def finish_inner(self):
+        def sent(i):
+            self.across_copy(i).wait_send()
+            self.back_copy(i).wait_send()
+
+        self.each(self.inner, sent)
+
+    def finish(self):
+        self.finish_inner()
+        self.finish_ends()
 
 
 def quotient(a, b):
@@ -877,6 +891,7 @@
     gather_out.finish()
     low = attended[...].astype(jnp.bfloat16)
     each = term.shape[2]
+    line = LineSum(term, passing, total, chain_sems, 2, second=3)
 
     @pl.loop(0, count)
     def _(k):
@@ -886,12 +901,12 @@
         )
         term[2 * k] = made[:, :each]
         term[2 * k + 1] = made[:, each:]
-
+        line.send(2 * k, 2)
+
+    line.send(2 * count, 2 * count)
     store(out_here, out_full)
 
     down.start()
-    line = LineSum(term, passing, total, chain_sems, 2)
-    line.send(0, line.count)
     relays = [
         (at, at, 1, lambda _, job=job: job())
         for at, job in (
@@ -910,8 +925,7 @@
         by_step(now, relays)
         line.step(now)
 
-    line.receive_all()
-    store(total, attn_sum)
+    collected = line.collect(attn_sum, load_sems.at[3])
     down.finish_relay()
     line.finish()
     for part in (gate_one, gate_two, up, down):
@@ -930,6 +944,7 @@
 
     for copy in stores:
         copy.wait()
+    collected.wait()
 
 
 def attend(
@@ -1001,7 +1016,7 @@
             pltpu.SemaphoreType.DMA((2, 3)),
             pltpu.SemaphoreType.DMA((4, 4 * count)),
             pltpu.SemaphoreType.DMA((len(out_shape),)),
-            pltpu.SemaphoreType.DMA((3,)),
+            pltpu.SemaphoreType.DMA((4,)),
         ],
         compiler_params=pltpu.CompilerParams(
             collective_id=0, has_side_effects=True, vmem_limit_bytes=VMEM_BYTES
@@ -1186,7 +1201,7 @@
                 )
         return found
 
-    ahead = 3
+    ahead = 4
 
     def mid_pair(n, row):
         cut = pl.ds(pl.multiple_of(n * 2 * each, 2 * each), 2 * each)
@@ -1347,8 +1362,6 @@
 
     gate_sum.finish(grad_gate)
     store(grad_gate, grad_gate_out)
-    line.receive_all()
-    store(total, back_sum)
     @pl.when(line.inner)
     def _():
         for c in range(lead):
@@ -1363,6 +1376,7 @@
     store(own_up.at[0], up_out.at[pl.ds(0, span), :])
     store(own_up.at[2, pl.ds(0, rows)], up_out.at[pl.ds(span, rows), :])
     store(own_up.at[1, pl.ds(rows, rows)], up_out.at[pl.ds(span + rows, rows), :])
+    collected = line.collect(back_sum, store_sems.at[7])
     line.finish()
     for part in range(2):
         for copy in swaps_of(part):
@@ -1383,6 +1397,7 @@
 
     for copy in stores:
         copy.wait()
+    collected.wait()
 
 
 def feed(chain, small_all, x, attn_sum, cotangent, gate_full, up_full, down_full):
@@ -1523,7 +1538,7 @@
             token_device(flip),
         )
 
-    mlp_line = LineSum(mlp_sum, mlp_passing, mlp_total, mlp_sems, given=LEAD)
+    mlp_line = LineSum(mlp_sum, mlp_passing, mlp_total, mlp_sems, given=LEAD, second=LEAD + 1)
     load_mlp.wait()
     mlp_line.start_given()
     mlp_line.send(LEAD, 2 * count - LEAD)
@@ -1567,7 +1582,7 @@
     summed_here[...] = jnp.broadcast_to(mean, summed_here.shape)
     for flip in range(1, 8):
         gain_copy(1, mid_part, flip).start()
-    mlp_line.step(LineSum.SECOND)
+    mlp_line.step(mlp_line.second)
     load_up.wait()
     for slot in range(2):
         up_copy(slot).start()
@@ -1583,7 +1598,7 @@
                 jnp.bfloat16
             )
 
-    mlp_line.step(LineSum.SECOND + 1)
+    mlp_line.step(mlp_line.second + 1)
     load_attended.wait()
     att_low[mine, :] = attended[...].astype(jnp.bfloat16)
     swap_back = swap(0, back_attn)
@@ -1610,7 +1625,7 @@
     load_out.wait()
     back_att[...] = nt_dot(back_attn[mine, :], out_here[...]).astype(jnp.bfloat16)
     swap_cot = swap(2, cotangents)
-    mlp_line.step(LineSum.SECOND + 2)
+    mlp_line.step(mlp_line.second + 2)
     load_hidden.wait()
     swap_hidden = swap(3, hidden)
 
@@ -1632,12 +1647,13 @@
                 used, both, own_marks + split_marks(jnp.broadcast_to(-peak, lane.shape), at)
             ).astype(jnp.bfloat16)
 
+    mlp_line.step(mlp_line.second + 3)
     load_normed.wait()
     swap_normed = swap(4, normed)
     load_in.wait()
     load_pair.wait()
 
-    begun = LineSum.SECOND + 3
+    begun = mlp_line.second + 4
     back_rows[...] = jnp.zeros_like(back_rows)
 
     def key_step(k, diagonal):
@@ -1913,7 +1929,7 @@
         gain_copy(0, pre_part, flip).start()
     mean = jnp.sum(weighed[...], axis=1, keepdims=True) / width
     weighed[...] = jnp.broadcast_to(mean, weighed.shape)
-    line.finish()
+    line.finish_ends()
 
     @pl.loop(0, 2 * count)
     def _(c):
@@ -1933,6 +1949,7 @@
     for flip in range(1, 8):
         for which, src in enumerate((pre_part, mid_part)):
             gain_copy(which, src, flip).wait_send()
+    line.finish_inner()
     for copy in (swap_back, swap_att, swap_hidden, swap_normed, swap_all):
         copy.wait_send()
 
@@ -2110,7 +2127,10 @@
     query_width = query_weight.shape[1]
     heads_here = query_width // head_size
     places = ROW // row_count
-    gains = jnp.concatenate([pre_gain, mid_gain]).astype(jnp.float32)[None]
+    half = pre_gain.shape[0]
+    gains = jnp.pad(pre_gain.astype(jnp.float32), (0, half)) + jnp.pad(
+        mid_gain.astype(jnp.float32), (half, 0)
+    )
     half_size = head_size // 2
     inverse = 10000.0 ** (-np.arange(half_size, dtype=np.float32) / half_size)
     inverse = jnp.asarray(np.tile(inverse.astype(np.float32), (8, 128 // half_size)))
@@ -2135,7 +2155,7 @@
         places,
         inputs,
         segments[None],
-        gains,
+        gains[None],
         key_weight,
         value_weight,
         inverse,

time: 306 us -> 298 us (0.974)
  Pallas kernels: 303 us -> 295 us
    pallas_call x1, Pallas kernels: 77.2 us -> 71.3 us  [feed(): pl.pallas_call(functools.partial(feed_kernel, chain), out_shape=[shape(at...]
where the time goes in v2:
time: 298 us
  Pallas kernels  295 us (99%)
    pallas_call x1, Pallas kernels, way_back(): pl.pallas_call(functools.partial(return_kernel, chain, places), out_shape...  113 us
    pallas_call x1, Pallas kernels, attend(): pl.pallas_call(functools.partial(attend_kernel, chain, places), out_shape...  105 us
    pallas_call x1, Pallas kernels, feed(): pl.pallas_call(functools.partial(feed_kernel, chain), out_shape=[shape(at...  71.3 us
    pallas_call x1, Pallas kernels, hand_over(): pl.pallas_call(functools.partial(hand_over_kernel, count), out_shape=[jax...  6.99 us

profile of v2, /device:TPU:0, one launch (start us, length us, event | category | flops | bytes accessed | tf_op | source)
XLA Modules:
  0.0 297.6 jit_solution(306266024584802253)
XLA Ops:
  0.6 1.3 convert_add_fusion
  1.9 104.5 %attend_forward.1 = (bf16[2048,1408]{1,0:T(8,128)(2,1)}, bf16[2048,1408]{1,0:T(8,128)(2,1)}, bf16[1408,2048]{1,0:T(8,128)(2,1)}, bf16[2048,512]{1,0:T(8,128)(2,1...) custom-call(bf16[512,2048]{1,0:T(8,128)(2,1)} %x_in.3, ...), custom_call_target="tpu_custom_call" | custom-call | tf_op jit(solution)/shard_map/attend_forward/pallas_call | solution.py:981
  106.4 71.3 %feed_forward.1 = (bf16[16,512,128]{2,1,0:T(8,128)(2,1)}, bf16[512,1408]{1,0:T(8,128)(2,1)}, bf16[16,512,128]{2,1,0:T(8,128)(2,1)}, f32[512,128]{1,0:T(8,128)}, ...) custom-call(f32[8,8,512]{2,1,0:T(8,128)} %get-tuple-element.52.small_all, bf16[512,2048]{1,0:T(8,128)(2,1)} %x_in.3, ...), custom_call_target="tpu_custom_call" | custom-call | tf_op jit(solution)/shard_map/feed_forward/pallas_call | solution.py:1412
  177.7 112.7 %way_back.1 = (bf16[512,2048]{1,0:T(8,128)(2,1)}, bf16[512,2048]{1,0:T(8,128)(2,1)}, bf16[1408,256]{1,0:T(8,128)(2,1)}, bf16[256,512]{1,0:T(8,128)(2,1)}, f32[64...) custom-call(f32[8,8,512]{2,1,0:T(8,128)} %get-tuple-element.52.small, ...), custom_call_target="tpu_custom_call" | custom-call | tf_op jit(solution)/shard_map/way_back/pallas_call | solution.py:1982
  290.4 7.0 %hand_over.1 = (bf16[512,2048]{1,0:T(8,128)(2,1)}, bf16[512,2048]{1,0:T(8,128)(2,1)}, f32[256,512]{1,0:T(8,128)}, f32[64,256]{1,0:T(8,128)}, f32[64,256]{1,0:T(8...) custom-call(f32[8,512]{1,0:T(8,128)} %get-tuple-element.72.gains, ...), custom_call_target="tpu_custom_call" | custom-call | tf_op jit(solution)/shard_map/hand_over/pallas_call | solution.py:2092

commit v3 on v2

--- a/solution.py
+++ b/solution.py
@@ -625,9 +625,9 @@
 
 
 def attend_kernel(
-    chain, places, x, ids, gains, key_shard, value_shard, inverse, query_shard, out_shard, gate_shard, up_shard,
+    chain, places, x_in, ids, gains, key_shard, value_shard, inverse, query_shard, out_shard, gate_shard, up_shard,
     down_shard, gate_full, up_full, down_full, query_full, pair_full, out_full, attn_sum, normed_out, query_out,
-    pairs, attended_out, log_out, cos_out, sin_out, small_out, small, gate_here, up_here, down_here, small_all, query_here, pair_here, pair_shard,
+    pairs, attended_out, log_out, cos_out, sin_out, small_out, x, small, gate_here, up_here, down_here, small_all, query_here, pair_here, pair_shard,
     out_here, pre_row, normed, query, attended, log_total, cos_table, sin_table, key_side, value_side, marks,
     scores, peak, mixed, near_pairs, term, passing, total, small_sems, gather_sems, local_sems, pair_sems,
     chain_sems, store_sems, load_sems,
@@ -638,6 +638,8 @@
     me = lax.axis_index("tokens")
     place = lax.rem(me, places)
     far = place >= 2
+    load_x = pltpu.make_async_copy(x_in, x, load_sems.at[4])
+    load_x.start()
     loads = [
         pltpu.make_async_copy(src, dst, load_sems.at[k])
         for k, (src, dst) in enumerate(
@@ -691,6 +693,7 @@
     gather_pair.start()
     gather_query.start()
     small_all[me] = small[...]
+    load_x.wait()
     x_f = x[...].astype(jnp.float32)
     pre_scale = lax.rsqrt(jnp.mean(x_f * x_f, axis=1, keepdims=True) + 1e-05)
 
@@ -981,9 +984,10 @@
     return pl.pallas_call(
         functools.partial(attend_kernel, chain, places),
         out_shape=out_shape,
-        in_specs=[vmem] * 6 + [anywhere] * 5,
+        in_specs=[anywhere] + [vmem] * 5 + [anywhere] * 5,
         out_specs=[anywhere] * len(out_shape),
         scratch_shapes=[
+            pltpu.VMEM((tokens, width), bf16),
             pltpu.VMEM(small, f32),
             pltpu.VMEM(gate_weight.shape, bf16),
             pltpu.VMEM(up_weight.shape, bf16),
@@ -1016,7 +1020,7 @@
             pltpu.SemaphoreType.DMA((2, 3)),
             pltpu.SemaphoreType.DMA((4, 4 * count)),
             pltpu.SemaphoreType.DMA((len(out_shape),)),
-            pltpu.SemaphoreType.DMA((4,)),
+            pltpu.SemaphoreType.DMA((5,)),
         ],
         compiler_params=pltpu.CompilerParams(
             collective_id=0, has_side_effects=True, vmem_limit_bytes=VMEM_BYTES
@@ -1466,13 +1470,14 @@
 
 
 def return_kernel(
-    chain, places, small_all, query, pairs, log_total, cos_table, sin_table, scale,
+    chain, places, small_in, query_in, pairs_in, log_in, cos_in, sin_in, scale_in,
     attended_in, x_in, attn_in, back_sum, query_full, pair_full, out_full, mlp_term, hidden_in, cotangent, normed_in, up_in, layer_out, grad_input, grad_down_out,
     grad_query, grad_key, grad_value, grad_out_out, grad_up_out, gains, mid_part, grad_down, grad_out, pair_back, grad_in, in_here, out_here, key_side, value_side, query_side, back_side, back_att,
     back_rows, back_keys, back_values, pair_out, pair_near, normed, back_attn, hidden, cotangents, att_low,
     back_all, pre_row, pre_part, gains_near, mlp_sum, mlp_passing, mlp_total, term, passing, total, own_down,
     near_down, own_in, near_in, own_out, near_out, load_sems, swap_sems, pair_sems, gain_sems, mlp_sems, chain_sems,
-    reduce_sems, store_sems, up_half, up_near, up_sems,
+    reduce_sems, store_sems, up_half, up_near, up_sems, small_all, query, pairs, log_total, cos_table, sin_table, scale,
+    table_sems,
 ):
     count = term.shape[0] // 2
     each = term.shape[2]
@@ -1490,6 +1495,22 @@
         return copy
 
     load_mlp = load(5, mlp_term, mlp_sum)
+    tables = [
+        pltpu.make_async_copy(src, dst, table_sems.at[k])
+        for k, (src, dst) in enumerate(
+            (
+                (small_in, small_all),
+                (scale_in, scale),
+                (query_in, query),
+                (pairs_in, pairs),
+                (log_in, log_total),
+                (cos_in, cos_table),
+                (sin_in, sin_table),
+            )
+        )
+    ]
+    for table in tables:
+        table.start()
     load_cot = load(2, cotangent, cotangents.at[mine, :])
     attended = back_rows
     load_attended = load(7, attended_in, attended)
@@ -1553,6 +1574,8 @@
             token_device((4, 2)[slot]),
         )
 
+    tables[0].wait()
+    tables[1].wait()
     for k in range(8):
         pre_row[:, k * span : (k + 1) * span] = jnp.broadcast_to(
             small_all[k, 1:2, span : 2 * span], (8, span)
@@ -1604,6 +1627,8 @@
     swap_back = swap(0, back_attn)
     swap_att = swap(1, att_low)
 
+    for table in tables[2:]:
+        table.wait()
     lane = lanes((tokens, 128))
     at = lane % 64
     first_id = (first_device // places * 4).astype(jnp.float32)
@@ -1992,7 +2017,7 @@
             shape((span, inner), bf16),
             shape((8, 2 * span), f32),
         ],
-        in_specs=[vmem] * 7 + [anywhere] * 12,
+        in_specs=[anywhere] * 19,
         out_specs=[anywhere] * 8 + [vmem],
         scratch_shapes=[
             pltpu.VMEM((8, width), f32),
@@ -2044,6 +2069,14 @@
             pltpu.VMEM((2 * span, inner), bf16),
             pltpu.VMEM((2, span // 2, inner), bf16),
             pltpu.SemaphoreType.DMA((2, 2)),
+            pltpu.VMEM(small_all.shape, f32),
+            pltpu.VMEM(query.shape, bf16),
+            pltpu.VMEM(pairs.shape, bf16),
+            pltpu.VMEM(log_total.shape, f32),
+            pltpu.VMEM(cos_table.shape, f32),
+            pltpu.VMEM(sin_table.shape, f32),
+            pltpu.VMEM(scale.shape, f32),
+            pltpu.SemaphoreType.DMA((7,)),
         ],
         compiler_params=pltpu.CompilerParams(
             collective_id=2, has_side_effects=True, vmem_limit_bytes=VMEM_BYTES

time: 298 us -> 296 us (level)
  no operation moved by 1% of the time
where the time goes in v3:
time: 296 us; the launch traced here: 295 us
  Pallas kernels  293 us (99%)
    pallas_call x1, Pallas kernels, way_back(): pl.pallas_call(functools.partial(return_kernel, chain, places), out_shape...  111 us
    pallas_call x1, Pallas kernels, attend(): pl.pallas_call(functools.partial(attend_kernel, chain, places), out_shape...  104 us
    pallas_call x1, Pallas kernels, feed(): pl.pallas_call(functools.partial(feed_kernel, chain), out_shape=[shape(at...  71.3 us
    pallas_call x1, Pallas kernels, hand_over(): pl.pallas_call(functools.partial(hand_over_kernel, count), out_shape=[jax...  6.99 us

profile of v3, /device:TPU:0, one launch (start us, length us, event | category | flops | bytes accessed | tf_op | source)
XLA Modules:
  0.0 295.2 jit_solution(24907263283106460)
XLA Ops:
  0.6 1.3 convert_add_fusion
  1.9 103.7 %attend_forward.1 = (bf16[2048,1408]{1,0:T(8,128)(2,1)}, bf16[2048,1408]{1,0:T(8,128)(2,1)}, bf16[1408,2048]{1,0:T(8,128)(2,1)}, bf16[2048,512]{1,0:T(8,128)(2,1...) custom-call(bf16[512,2048]{1,0:T(8,128)(2,1)} %x_in.5, ...), custom_call_target="tpu_custom_call" | custom-call | tf_op jit(solution)/shard_map/attend_forward/pallas_call | solution.py:984
  105.6 71.3 %feed_forward.1 = (bf16[16,512,128]{2,1,0:T(8,128)(2,1)}, bf16[512,1408]{1,0:T(8,128)(2,1)}, bf16[16,512,128]{2,1,0:T(8,128)(2,1)}, f32[512,128]{1,0:T(8,128)}, ...) custom-call(f32[8,8,512]{2,1,0:T(8,128)} %get-tuple-element.52.small_all.small_in, bf16[512,2048]{1,0:T(8,128)(2,1)} %x_in.5, ...), custom_call_target="tpu_custom_call" | custom-call | tf_op jit(solution)/shard_map/feed_forward/pallas_call | solution.py:1416
  176.9 111.1 %way_back.1 = (bf16[512,2048]{1,0:T(8,128)(2,1)}, bf16[512,2048]{1,0:T(8,128)(2,1)}, bf16[1408,256]{1,0:T(8,128)(2,1)}, bf16[256,512]{1,0:T(8,128)(2,1)}, f32[64...) custom-call(f32[8,8,512]{2,1,0:T(8,128)} %get-tuple-element.52.small, ...), custom_call_target="tpu_custom_call" | custom-call | tf_op jit(solution)/shard_map/way_back/pallas_call | solution.py:2007
  288.1 7.0 %hand_over.1 = (bf16[512,2048]{1,0:T(8,128)(2,1)}, bf16[512,2048]{1,0:T(8,128)(2,1)}, f32[256,512]{1,0:T(8,128)}, f32[64,256]{1,0:T(8,128)}, f32[64,256]{1,0:T(8...) custom-call(f32[8,512]{1,0:T(8,128)} %get-tuple-element.72.gains, ...), custom_call_target="tpu_custom_call" | custom-call | tf_op jit(solution)/shard_map/hand_over/pallas_call | solution.py:2125
